TPU v7x, 128 devices: a whole 4x4x4 slice. The times are simulated.
128 devices in a mesh: dp: 4 (over x), ex: 8 (over z, core), ey: 4 (over y).
Axes of the slice: x: 4, y: 4, z: 4, core: 2. Of those that a mesh axis runs over, the one named last changes fastest.
Arguments:
- tokens: bfloat16 [16384, 2048], P(('dp', 'ex', 'ey')), may hold values from -6 to 6
- out_grad: bfloat16 [16384, 2048], P(('dp', 'ex', 'ey')), may hold values from -0.59765625 to 0.59765625
- router_logits: float32 [16384, 128], P(('dp', 'ex', 'ey')), may hold values from -16 to 306
- expert_picks: int32 [16384, 8], P(('dp', 'ex', 'ey')), may hold values from 0 to 127, all different within a row; in each aligned block of 128 rows (0 to 127, 128 to 255, ...) at most 9 rows name the same one
- micro_batch: int32 [16384], P(('dp', 'ex', 'ey')), may hold values from 0 to 1
- w_gate: bfloat16 [128, 2048, 768], P(('dp', 'ex', 'ey'))
- w_up: bfloat16 [128, 2048, 768], P(('dp', 'ex', 'ey'))
- w_down: bfloat16 [128, 768, 2048], P(('dp', 'ex', 'ey'))
Outputs:
- grad_tokens: bfloat16 [16384, 2048], P(('dp', 'ex', 'ey'))
- grad_logits: float32 [16384, 128], P(('dp', 'ex', 'ey'))
- balance_grad: float32 [16384, 128], P(('dp', 'ex', 'ey'))
- grad_gate: bfloat16 [128, 2048, 768], P(('dp', 'ex', 'ey'))
- grad_up: bfloat16 [128, 2048, 768], P(('dp', 'ex', 'ey'))
- grad_down: bfloat16 [128, 768, 2048], P(('dp', 'ex', 'ey'))
Inputs may be any that keep to these rules, and one draw needn't show every extreme that they name: `expert_picks`: each token names 8 different experts; among the tokens of one device no expert is named more than 9 times, and some expert of some device is named exactly 9 times.
All inputs are finite; a program needn't handle non-finite values.
Results may differ from a plain program's by a relative error of at most 0.02.
Values may be sent and summed in bfloat16 or wider, within the bound.
A program may use at most 128 MiB of HBM per device.

v0:
```python
import jax
import jax.numpy as jnp
from jax import lax
from jax.sharding import PartitionSpec as P

MICRO = 2


contract_rows = (((0,), (0,)), ((), ()))
contract_cols = (((1,), (1,)), ((), ()))


def silu_parts(pre_gate):
    logistic = jax.nn.sigmoid(pre_gate)
    return (pre_gate * logistic, logistic * (1.0 + pre_gate * (1.0 - logistic)))


def expert_backward(token_rows, cotangent_rows, weight_rows, gate_matrix, up_matrix, down_matrix):
    pre_gate = jnp.dot(token_rows, gate_matrix, preferred_element_type=jnp.float32)
    pre_up = jnp.dot(token_rows, up_matrix, preferred_element_type=jnp.float32)
    activation, derivative = silu_parts(pre_gate)
    hidden = (activation * pre_up).astype(jnp.bfloat16)
    back_hidden = lax.dot_general(
        cotangent_rows, down_matrix, contract_cols, preferred_element_type=jnp.float32
    )
    scores = jnp.sum(hidden.astype(jnp.float32) * back_hidden, axis=1).astype(jnp.bfloat16)
    scaled_out = (weight_rows[:, None] * cotangent_rows.astype(jnp.float32)).astype(jnp.bfloat16)
    grad_down = lax.dot_general(
        hidden, scaled_out, contract_rows, preferred_element_type=jnp.float32
    ).astype(jnp.bfloat16)
    hidden_grad = weight_rows[:, None] * back_hidden
    gate_grad = (hidden_grad * pre_up * derivative).astype(jnp.bfloat16)
    up_grad = (hidden_grad * activation).astype(jnp.bfloat16)
    grad_gate = lax.dot_general(
        token_rows, gate_grad, contract_rows, preferred_element_type=jnp.float32
    ).astype(jnp.bfloat16)
    grad_up = lax.dot_general(
        token_rows, up_grad, contract_rows, preferred_element_type=jnp.float32
    ).astype(jnp.bfloat16)
    pair_grad = lax.dot_general(
        gate_grad, gate_matrix, contract_cols, preferred_element_type=jnp.float32
    )
    pair_grad = pair_grad + lax.dot_general(
        up_grad, up_matrix, contract_cols, preferred_element_type=jnp.float32
    )
    return (pair_grad.astype(jnp.bfloat16), scores, grad_gate, grad_up, grad_down)


def per_device(tokens, out_grad, router_logits, expert_picks, micro_batch, w_gate, w_up, w_down):
    tok_rows, model_width = tokens.shape
    picks_each = expert_picks.shape[1]
    experts = router_logits.shape[1]
    capacity = tok_rows * picks_each * 9 // (8 * experts)
    pair_rows = tok_rows * picks_each
    expert_ids = jnp.arange(experts, dtype=jnp.int32)
    row_top = jnp.max(router_logits, axis=1, keepdims=True)
    exponent = jnp.exp(router_logits - row_top)
    probabilities = exponent / jnp.sum(exponent, axis=1, keepdims=True)
    picked = jnp.take_along_axis(router_logits, expert_picks, axis=1)
    picked_exp = jnp.exp(picked - jnp.max(picked, axis=1, keepdims=True))
    route_weight = picked_exp / jnp.sum(picked_exp, axis=1, keepdims=True)
    pick_match = expert_picks[:, :, None] == expert_ids
    pick_hot = jnp.sum(pick_match.astype(jnp.float32), axis=1)
    batch_hot = (micro_batch[:, None] == jnp.arange(MICRO, dtype=jnp.int32)).astype(jnp.float32)
    part_counts = lax.dot_general(
        batch_hot, pick_hot, contract_rows, precision=lax.Precision.HIGHEST
    )
    occupancy = lax.psum(part_counts, ("dp", "ex", "ey"))
    flat_picks = expert_picks.reshape(pair_rows)
    flat_hot = (flat_picks[:, None] == expert_ids).astype(jnp.int32)
    slot_rank = jnp.sum((jnp.cumsum(flat_hot, axis=0) - 1) * flat_hot, axis=1)
    slot_index = flat_picks * capacity + slot_rank
    holder = jnp.full((experts * capacity,), pair_rows, jnp.int32)
    holder = holder.at[slot_index].set(jnp.arange(pair_rows, dtype=jnp.int32))
    occupied = holder < pair_rows
    safe_pair = jnp.minimum(holder, pair_rows - 1)
    source_token = safe_pair // picks_each
    token_send = jnp.where(occupied[:, None], tokens[source_token], 0)
    token_send = token_send.reshape(experts, capacity, model_width)
    cotangent_send = jnp.where(occupied[:, None], out_grad[source_token], 0)
    cotangent_send = cotangent_send.reshape(experts, capacity, model_width)
    weight_send = jnp.where(occupied, route_weight.reshape(pair_rows)[safe_pair], 0.0).astype(
        jnp.bfloat16
    )
    weight_send = weight_send.reshape(experts, capacity)
    token_recv, cotangent_recv, weight_recv = (
        lax.all_to_all(token_send, ("dp", "ex", "ey"), split_axis=0, concat_axis=0, tiled=True),
        lax.all_to_all(cotangent_send, ("dp", "ex", "ey"), split_axis=0, concat_axis=0, tiled=True),
        lax.all_to_all(weight_send, ("dp", "ex", "ey"), split_axis=0, concat_axis=0, tiled=True),
    )
    pair_grads, scores, grad_gate, grad_up, grad_down = expert_backward(
        token_recv.reshape(experts * capacity, model_width),
        cotangent_recv.reshape(experts * capacity, model_width),
        weight_recv.reshape(experts * capacity).astype(jnp.float32),
        w_gate[0],
        w_up[0],
        w_down[0],
    )
    back_rows, back_scores = (
        lax.all_to_all(
            pair_grads.reshape(experts, capacity, model_width),
            ("dp", "ex", "ey"),
            split_axis=0,
            concat_axis=0,
            tiled=True,
        ),
        lax.all_to_all(
            scores.reshape(experts, capacity),
            ("dp", "ex", "ey"),
            split_axis=0,
            concat_axis=0,
            tiled=True,
        ),
    )
    back_rows = back_rows.reshape(experts * capacity, model_width)
    back_scores = back_scores.reshape(experts * capacity)
    pair_back = back_rows[slot_index].reshape(tok_rows, picks_each, model_width)
    grad_tokens = jnp.sum(pair_back.astype(jnp.float32), axis=1).astype(jnp.bfloat16)
    pair_scores = back_scores[slot_index].reshape(tok_rows, picks_each).astype(jnp.float32)
    mean_score = jnp.sum(route_weight * pair_scores, axis=1, keepdims=True)
    route_grad = route_weight * (pair_scores - mean_score)
    grad_logits = jnp.sum(jnp.where(pick_match, route_grad[:, :, None], 0.0), axis=1)
    load = occupancy * (experts * MICRO / (picks_each * tok_rows * experts))
    token_load = jnp.sum(batch_hot[:, :, None] * load[None, :, :], axis=1)
    mean_load = jnp.sum(probabilities * token_load, axis=1, keepdims=True)
    balance_grad = probabilities * (token_load - mean_load)
    return (grad_tokens, grad_logits, balance_grad, grad_gate[None], grad_up[None], grad_down[None])


def solution(mesh):
    placed = (
        P(("dp", "ex", "ey"), None),
        P(("dp", "ex", "ey"), None),
        P(("dp", "ex", "ey"), None),
        P(("dp", "ex", "ey"), None),
        P(("dp", "ex", "ey")),
        P(("dp", "ex", "ey"), None, None),
        P(("dp", "ex", "ey"), None, None),
        P(("dp", "ex", "ey"), None, None),
    )
    return jax.shard_map(
        per_device,
        mesh=mesh,
        in_specs=placed,
        out_specs=(
            P(("dp", "ex", "ey"), None),
            P(("dp", "ex", "ey"), None),
            P(("dp", "ex", "ey"), None),
            P(("dp", "ex", "ey"), None, None),
            P(("dp", "ex", "ey"), None, None),
            P(("dp", "ex", "ey"), None, None),
        ),
        check_vma=False,
    )
```

profile of v0, /device:TPU:1, one launch (start us, length us, event | category | flops | bytes accessed | tf_op | source)
XLA Modules:
  0.0 585.1 jit_solution(14450158512702748564)
XLA Ops:
  5.5 4.3 scatter_custom_fusion
  10.1 11.8 %gather_fusion.2 = bf16[1152,2048]{1,0:T(8,128)(2,1)} fusion(bf16[128,2048]{1,0:T(8,128)(2,1)} %param.8, s32[2048]{0:T(1024)S(1)} %get-tuple-element.19), kind=kCustom, calls=%fused_computation.2 | custom fusion | bytes 9441792 | tf_op jit(solution)/shard_map/gather | solution.py:78
  21.9 8.0 %gather.28 = bf16[128,9,2048]{2,1,0:T(8,128)(2,1)} reshape(bf16[1152,2048]{1,0:T(8,128)(2,1)} %gather_fusion.2) | data formatting | bytes 9437184 | tf_op jit(solution)/shard_map/gather | solution.py:78
  29.9 11.8 %gather_fusion.1 = bf16[1152,2048]{1,0:T(8,128)(2,1)} fusion(bf16[128,2048]{1,0:T(8,128)(2,1)} %param.9, s32[2048]{0:T(1024)S(1)} %get-tuple-element.19), kind=kCustom, calls=%fused_computation.1 | custom fusion | bytes 9441792 | tf_op jit(solution)/shard_map/gather | solution.py:80
  41.7 8.1 %gather.26 = bf16[128,9,2048]{2,1,0:T(8,128)(2,1)} reshape(bf16[1152,2048]{1,0:T(8,128)(2,1)} %gather_fusion.1) | data formatting | bytes 9437184 | tf_op jit(solution)/shard_map/gather | solution.py:80
  49.8 9.2 %broadcast_select_fusion.1 = (bf16[128,9,2048]{2,1,0:T(8,128)(2,1)}, bf16[128,9,2048]{2,1,0:T(8,128)(2,1)S(1)}) fusion(bf16[128,9,2048]{2,1,0:T(8,128)(2,1)} %gather.26, pred[128,9]{1,0:T(8,128)(4,1)S(1)} %broadcast_in_dim.78, bf16[128,9,2048]{2,1,0:T(8,128)(2,1)} %gather.28), kind=kLoop, calls=%fused_computation.10 | loop fusion | flops 4718592 | bytes 18875520 | tf_op jit(solution)/shard_map/jit(_where)/select_n | solution.py:80
  59.0 109.9 %all_to_all.31 = bf16[128,9,2048]{2,1,0:T(8,128)(2,1)} all-to-all(bf16[128,9,2048]{2,1,0:T(8,128)(2,1)S(1)} %get-tuple-element.15), channel_id=1, replica_groups=mesh['dp'=4,'ex'=8,'ey'=4] {'dp','ex','ey'}, dimensions={0} | all-to-all | bytes 9437184 | tf_op jit(solution)/shard_map/all_to_all | solution.py:87
  168.8 7.5 %all-to-all-start.1 = ((bf16[128,9,2048]{2,1,0:T(8,128)(2,1)}), bf16[128,9,2048]{2,1,0:T(8,128)(2,1)}, u32[]{:S(2)}, u32[]{:S(2)}) async-start(bf16[128,9,2048]{2,1,0:T(8,128)(2,1)} %get-tuple-element.14), calls=%async_computation.1 | async-start | bytes 16777216 | tf_op jit(solution)/shard_map/all_to_all | solution.py:88
  177.2 6.8 %gather_fusion.5 = f32[1024]{0:T(1024)S(1)} fusion(f32[128,128]{1,0:T(8,128)S(1)} %copy-done.1, s32[1024]{0:T(1024)S(1)} %reshape.251), kind=kCustom, calls=%fused_computation.5 | custom fusion | bytes 16384 | tf_op jit(solution)/shard_map/jit(take_along_axis)/gather | solution.py:59
  184.2 8.4 %reshape.204 = bf16[1152,2048]{1,0:T(8,128)(2,1)} reshape(bf16[128,9,2048]{2,1,0:T(8,128)(2,1)} %all_to_all.31) | data formatting | bytes 9437184 | tf_op jit(solution)/shard_map/reshape | solution.py:92
  192.7 8.6 %fusion.6 = f32[1152,768]{0,1:T(8,128)} fusion(bf16[1152,2048]{1,0:T(8,128)(2,1)} %reshape.204, bf16[1,2048,768]{2,1,0:T(8,128)(2,1)S(1)} %copy-done), kind=kOutput, calls=%fused_computation.25 | convolution fusion | flops 3623878656 | bytes 11403264 | tf_op jit(solution)/shard_map/dot_general | solution.py:19
  201.3 6.4 %fusion.9 = f32[1152,768]{0,1:T(8,128)} fusion(bf16[1152,2048]{1,0:T(8,128)(2,1)S(1)} %copy-done.2, bf16[1,2048,768]{2,1,0:T(8,128)(2,1)S(1)} %copy-done.9), kind=kOutput, calls=%fused_computation.28 | convolution fusion | flops 3623878656 | bytes 11403264 | tf_op jit(solution)/shard_map/dot_general | solution.py:20
  207.7 73.3 %all-to-all-done.1 = bf16[128,9,2048]{2,1,0:T(8,128)(2,1)} async-done(((bf16[128,9,2048]{2,1,0:T(8,128)(2,1)}), bf16[128,9,2048]{2,1,0:T(8,128)(2,1)}, u32[]{:S(2)}, u32[]{:S(2)}) %all-to-all-start.1) | async-done | bytes 4718624 | tf_op jit(solution)/shard_map/all_to_all | solution.py:88
  281.0 8.7 %reshape.203 = bf16[1152,2048]{1,0:T(8,128)(2,1)} reshape(bf16[128,9,2048]{2,1,0:T(8,128)(2,1)} %all-to-all-done.1) | data formatting | bytes 9437184 | tf_op jit(solution)/shard_map/reshape | solution.py:93
  289.7 12.2 %multiply_reduce_fusion = (bf16[1152]{0:T(1024)(128)(2,1)S(1)}, bf16[1152,768]{0,1:T(8,128)(2,1)}, f32[1152,768]{0,1:T(8,128)}) fusion(f32[1152,768]{0,1:T(8,128)} %fusion.9, f32[1152,768]{0,1:T(8,128)} %fusion.6, bf16[1152,2048]{1,0:T(8,128)(2,1)} %reshape.203, bf16[1,768,2048]{2,1,0:T(8,128)(2,1)} %param.15), kind=kOutput, calls=%fused_computation.14 | convolution fusion | flops 3631840256 | bytes 20252928 | tf_op jit(solution)/shard_map/dot_general | solution.py:23
  302.8 6.3 %all-to-all-start.4 = ((bf16[128,1,9]{2,1,0:T(2,128)(2,1)}), bf16[128,1,9]{2,1,0:T(2,128)(2,1)S(1)}, u32[]{:S(2)}, u32[]{:S(2)}) async-start(bf16[128,1,9]{2,1,0:T(2,128)(2,1)} %convert_element_type.107), calls=%async_computation.4 | async-start | bytes 131072 | tf_op jit(solution)/shard_map/all_to_all | solution.py:107
  309.1 9.8 %all-to-all-done.4 = bf16[128,1,9]{2,1,0:T(2,128)(2,1)S(1)} async-done(((bf16[128,1,9]{2,1,0:T(2,128)(2,1)}), bf16[128,1,9]{2,1,0:T(2,128)(2,1)S(1)}, u32[]{:S(2)}, u32[]{:S(2)}) %all-to-all-start.4) | async-done | bytes 2336 | tf_op jit(solution)/shard_map/all_to_all | solution.py:107
  319.3 6.8 %gather_fusion.4 = bf16[1024]{0:T(1024)(128)(2,1)S(1)} fusion(bf16[1152]{0:T(1024)(128)(2,1)S(1)} %reshape.208, s32[1024]{0:T(1024)S(1)} %broadcast_clamp_fusion), kind=kCustom, calls=%fused_computation.4 | custom fusion | bytes 8192 | tf_op jit(solution)/shard_map/gather | solution.py:119
  326.5 7.3 %gather_fusion = bf16[1152]{0:T(1024)(128)(2,1)S(1)} fusion(bf16[1024]{0:T(1024)(128)(2,1)S(1)} %div.39, s32[2048]{0:T(1024)S(1)} %get-tuple-element.20), kind=kCustom, calls=%fused_computation | custom fusion | bytes 9216 | tf_op jit(solution)/shard_map/gather | solution.py:82
  334.1 14.0 %all_to_all.32 = bf16[128,1,9]{2,1,0:T(2,128)(2,1)S(1)} all-to-all(bf16[128,1,9]{2,1,0:T(2,128)(2,1)S(1)} %all_to_all.25), channel_id=1, replica_groups=mesh['dp'=4,'ex'=8,'ey'=4] {'dp','ex','ey'}, dimensions={0} | all-to-all | bytes 4608 | tf_op jit(solution)/shard_map/all_to_all | solution.py:89
  348.4 5.0 multiply_convert_fusion.3
  353.5 3.9 fusion.4
  357.4 5.7 add_convert_fusion
  363.1 8.1 %reshape.205 = bf16[128,9,2048]{2,1,0:T(8,128)(2,1)} reshape(bf16[1152,2048]{1,0:T(8,128)(2,1)} %add_convert_fusion) | data formatting | bytes 9437184 | tf_op jit(solution)/shard_map/reshape | solution.py:101
  371.3 5.2 all-to-all-start.3
  378.0 156.1 %psum.7 = f32[2,128]{1,0:T(2,128)S(1)} all-reduce(f32[2,128]{1,0:T(2,128)S(1)} %fusion.28), channel_id=1, replica_groups=mesh['dp'=4,'ex'=8,'ey'=4] {'dp','ex','ey'}, use_global_device_ids=true, to_apply=%region_13.14 | all-reduce | flops 256 | bytes 2048 | tf_op jit(solution)/shard_map/psum | solution.py:68
  535.1 9.0 %fusion.14 = bf16[1,2048,768]{2,1,0:T(8,128)(2,1)} fusion(bf16[1152,2048]{1,0:T(8,128)(2,1)} %reshape.204, bf16[1152,768]{0,1:T(8,128)(2,1)} %copy-done.6), kind=kOutput, calls=%fused_computation.33 | convolution fusion | flops 3625451520 | bytes 9633792 | tf_op jit(solution)/shard_map/dot_general | solution.py:37
  544.2 8.3 %fusion.13 = bf16[1,2048,768]{2,1,0:T(8,128)(2,1)} fusion(bf16[1152,2048]{1,0:T(8,128)(2,1)} %reshape.204, bf16[1152,768]{0,1:T(8,128)(2,1)S(1)} %copy-done.5), kind=kOutput, calls=%fused_computation.32 | convolution fusion | flops 3625451520 | bytes 9633792 | tf_op jit(solution)/shard_map/dot_general | solution.py:34
  552.5 5.8 fusion.15
  558.3 8.4 %reshape.206 = bf16[1152,2048]{1,0:T(8,128)(2,1)} reshape(bf16[128,9,2048]{2,1,0:T(8,128)(2,1)} %all-to-all-done.3) | data formatting | bytes 9437184 | tf_op jit(solution)/shard_map/reshape | solution.py:115
  566.7 12.0 %gather_fusion.3 = bf16[1024,2048]{1,0:T(8,128)(2,1)} fusion(bf16[1152,2048]{1,0:T(8,128)(2,1)} %reshape.206, s32[1024]{0:T(1024)S(1)} %broadcast_clamp_fusion), kind=kCustom, calls=%fused_computation.3 | custom fusion | bytes 8392704 | tf_op jit(solution)/shard_map/gather | solution.py:117
  578.8 5.9 %bitcast_reduce_fusion = bf16[128,2048]{1,0:T(8,128)(2,1)} fusion(bf16[1024,2048]{1,0:T(8,128)(2,1)} %gather_fusion.3), kind=kLoop, calls=%fused_computation.13 | loop fusion | flops 1835008 | bytes 4718592 | tf_op jit(solution)/shard_map/reduce_sum | solution.py:118
  (81 shorter events, 11.0 us)
Async XLA Ops:
  0.6 192.0 %copy-start = (bf16[1,2048,768]{2,1,0:T(8,128)(2,1)S(1)}, bf16[1,2048,768]{2,1,0:T(8,128)(2,1)}, u32[]{:S(2)}) copy-start(bf16[1,2048,768]{2,1,0:T(8,128)(2,1)} %param.13) | copy-start | bytes 9437188
  3.1 0.8 copy-start.3
  168.8 7.5 %copy-start.7 = (s32[128,8]{0,1:T(8,128)S(1)}, s32[128,8]{0,1:T(8,128)}, u32[]{:S(2)}) copy-start(s32[128,8]{0,1:T(8,128)} %param.11) | copy-start | bytes 12292
  168.8 112.1 %all-to-all-start.1 = ((bf16[128,9,2048]{2,1,0:T(8,128)(2,1)}), bf16[128,9,2048]{2,1,0:T(8,128)(2,1)}, u32[]{:S(2)}, u32[]{:S(2)}) async-start(bf16[128,9,2048]{2,1,0:T(8,128)(2,1)} %get-tuple-element.14), calls=%async_computation.1 | async-start | bytes 16777216 | tf_op jit(solution)/shard_map/all_to_all | solution.py:88
  176.4 0.8 copy-start.1
  192.7 8.6 %copy-start.2 = (bf16[1152,2048]{1,0:T(8,128)(2,1)S(1)}, bf16[1152,2048]{1,0:T(8,128)(2,1)}, u32[]{:S(2)}) copy-start(bf16[1152,2048]{1,0:T(8,128)(2,1)} %reshape.204) | copy-start | bytes 14155780
  192.7 8.6 %copy-start.9 = (bf16[1,2048,768]{2,1,0:T(8,128)(2,1)S(1)}, bf16[1,2048,768]{2,1,0:T(8,128)(2,1)}, u32[]{:S(2)}) copy-start(bf16[1,2048,768]{2,1,0:T(8,128)(2,1)} %param.14) | copy-start | bytes 9437188
  302.8 16.1 %all-to-all-start.4 = ((bf16[128,1,9]{2,1,0:T(2,128)(2,1)}), bf16[128,1,9]{2,1,0:T(2,128)(2,1)S(1)}, u32[]{:S(2)}, u32[]{:S(2)}) async-start(bf16[128,1,9]{2,1,0:T(2,128)(2,1)} %convert_element_type.107), calls=%async_computation.4 | async-start | bytes 131072 | tf_op jit(solution)/shard_map/all_to_all | solution.py:107
  353.4 4.0 copy-start.4
  353.4 4.0 copy-start.6
  353.5 4.0 copy-start.10
  371.3 5.5 copy-start.8
  371.3 187.0 %all-to-all-start.3 = ((bf16[128,9,2048]{2,1,0:T(8,128)(2,1)}), bf16[128,9,2048]{2,1,0:T(8,128)(2,1)}, u32[]{:S(2)}, u32[]{:S(2)}) async-start(bf16[128,9,2048]{2,1,0:T(8,128)(2,1)} %reshape.205), calls=%async_computation.3 | async-start | bytes 16777216 | tf_op jit(solution)/shard_map/all_to_all | solution.py:100
  535.1 9.1 %copy-start.5 = (bf16[1152,768]{0,1:T(8,128)(2,1)S(1)}, bf16[1152,768]{0,1:T(8,128)(2,1)}, u32[]{:S(2)}) copy-start(bf16[1152,768]{0,1:T(8,128)(2,1)} %copy-done.4) | copy-start | bytes 5308420
  535.1 17.3 %slice-start = ((s8[4718592]{0:T(1024)(128)(4,1)}), s8[4194304]{0:T(1024)(128)(4,1)S(1)}, s32[]{:S(2)}) async-start(s8[4718592]{0:T(1024)(128)(4,1)} %bitcast.49), calls=%async_computation.5 | async-start | bytes 8388608
  544.2 8.3 %slice-start.1 = ((s8[4718592]{0:T(1024)(128)(4,1)}), s8[524288]{0:T(1024)(128)(4,1)S(1)}, s32[]{:S(2)}) async-start(s8[4718592]{0:T(1024)(128)(4,1)} %bitcast.49), calls=%async_computation.6 | async-start | bytes 1048576
  544.2 8.3 %copy-start.11 = (bf16[1152,768]{0,1:T(8,128)(2,1)S(1)}, bf16[1152,768]{0,1:T(8,128)(2,1)}, u32[]{:S(2)}) copy-start(bf16[1152,768]{0,1:T(8,128)(2,1)} %get-tuple-element.11) | copy-start | bytes 5308420
where the time goes:
time: 593 us; the launch traced here: 585 us
  blocking collectives  280 us (47%)
  local copies, waits for them, and re-layouts  116 us (20%)
  waiting for transfers between devices  83.1 us (14%)
  matrix products  60.1 us (10%)
  other arithmetic  25.4 us (4%)
  starting transfers between devices  19 us (3%)
    psum x1, blocking collectives, per_device(): occupancy = lax.psum(part_counts, ('dp', 'ex', 'ey'))  156 us
    all_to_all x1, blocking collectives, per_device(): lax.all_to_all(token_send, ('dp', 'ex', 'ey'), split_axis=0, concat_axis=...  110 us
    all_to_all x1, waiting for transfers between devices, per_device(): lax.all_to_all(cotangent_send, ('dp', 'ex', 'ey'), split_axis=0, concat_a...  73.3 us
    gather x2, local copies, waits for them, and re-layouts, per_device(): token_send = jnp.where(occupied[:, None], tokens[source_token], 0)  19.8 us
    gather x2, local copies, waits for them, and re-layouts, per_device(): cotangent_send = jnp.where(occupied[:, None], out_grad[source_token], 0)  19.8 us
    all_to_all x1, blocking collectives, per_device(): lax.all_to_all(weight_send, ('dp', 'ex', 'ey'), split_axis=0, concat_axis...  14 us
    dot_general x1, matrix products, expert_backward(): lax.dot_general(cotangent_rows, down_matrix, contract_cols, preferred_ele...  12.2 us
    gather x1, local copies, waits for them, and re-layouts, per_device(): pair_back = back_rows[slot_index].reshape(tok_rows, picks_each, model_width)  12 us
  transfers between devices with their start and end apart: 3, of which 2 were waited for; matrix products, arithmetic and copies ran while one was open for 10% of the time, Pallas kernels for 0%

commit v1 on v0

v1 whole, which is shorter than its diff:
```python
import functools

import jax
import jax.numpy as jnp
from jax import lax
from jax.experimental import pallas as pl
from jax.experimental.pallas import tpu as pltpu
from jax.sharding import PartitionSpec as P

MESH = pl.DeviceIdType.MESH
F32, BF16, I32 = jnp.float32, jnp.bfloat16, jnp.int32
NN = (((1,), (0,)), ((), ()))
NT = (((1,), (1,)), ((), ()))
TN = (((0,), (0,)), ((), ()))

D, H, K, T, E, CAP, MICRO = 2048, 768, 8, 128, 128, 9, 2
CH = D // 128
MSG = CAP * CH
GROUPS = 4
PER = E // GROUPS
ROWS = PER * CAP
PAIRS = E * CAP
BLK = 32


def mm(a, b, dims):
    return lax.dot_general(a, b, dims, preferred_element_type=F32)


def offset(i):
    a, b, c, d = i % 4, (i // 4) % 4, (i // 16) % 4, i // 64
    dx, dy, dz = a, (a + b) % 4, (a + b + c) % 4
    return dx, dz, (a + b + c + d) % 2, dy


def shifted(i, sign):
    x, ex, y = lax.axis_index("dp"), lax.axis_index("ex"), lax.axis_index("ey")
    dx, dz, dc, dy = offset(i)
    return (
        (x + sign * dx + 4) % 4,
        (ex // 2 + sign * dz + 4) % 4 * 2 + (ex % 2 + dc) % 2,
        (y + sign * dy + 4) % 4,
    )


def rows_of(g, size):
    return pl.ds(pl.multiple_of(g * size, size), size)


def iota(shape, dim):
    return lax.broadcasted_iota(I32, shape, dim)


def kernel(
    tok_ref, cot_ref, logit_ref, pick_ref, mb_ref, wg_hbm, wu_hbm, wd_hbm,
    gt_ref, gl_ref, gb_ref, gg_hbm, gu_hbm, gd_hbm,
    sx, sc, rx, rc, ps, pr, xs, cs, hid, gu, wg, wu, wd, pg, hot, whot, code_rel, perm_ref, rwm_ref, prob_ref,
    qs, qr, acc, cnt, cnt_in, out_a, out_d,
    w_sem, sx_sem, sc_sem, rx_sem, rc_sem, ps_sem, pr_sem, qs_sem, qr_sem, cs_sem, cr_sem, oa_sem, od_sem,
):
    x, ex, y = lax.axis_index("dp"), lax.axis_index("ex"), lax.axis_index("ey")
    barrier = pltpu.get_barrier_semaphore()

    def greet(i, carry):
        pl.semaphore_signal(barrier, inc=1, device_id=shifted(i, 1), device_id_type=MESH)
        return carry

    lax.fori_loop(1, E, greet, 0)
    loads = [
        pltpu.make_async_copy(src, dst, w_sem.at[n])
        for n, (src, dst) in enumerate(((wg_hbm, wg), (wu_hbm, wu), (wd_hbm, wd)))
    ]
    for load in loads:
        load.start()

    expert_lane = iota((T, E), 1)
    picked = jnp.zeros((T, E), F32)
    for k in range(K):
        picked = jnp.where(pick_ref[:, k : k + 1] == expert_lane, 1.0, picked)
    logits = logit_ref[...]
    prob = jnp.exp(logits - jnp.max(logits, axis=1, keepdims=True))
    prob_ref[...] = prob / jnp.sum(prob, axis=1, keepdims=True)
    top = jnp.max(jnp.where(picked > 0.0, logits, -jnp.inf), axis=1, keepdims=True)
    rwm = jnp.where(picked > 0.0, jnp.exp(jnp.minimum(logits - top, 0.0)), 0.0)
    rwm = rwm / jnp.sum(rwm, axis=1, keepdims=True)
    rwm_ref[...] = rwm
    earlier = (iota((T, T), 1) < iota((T, T), 0)).astype(BF16)
    slot = mm(earlier, picked.astype(BF16), NN)
    code = jnp.where(picked > 0.0, slot, -1.0).astype(BF16)
    i_row = iota((E, E), 0)
    a, b, c, d = i_row & 3, (i_row >> 2) & 3, (i_row >> 4) & 3, i_row >> 6
    target = (
        ((x + a) & 3) * 32
        + (((ex // 2 + a + b + c) & 3) * 2 + ((ex % 2 + a + b + c + d) & 1)) * 4
        + ((y + a + b) & 3)
    )
    perm = (target == expert_lane).astype(BF16)
    perm_ref[...] = perm
    code_rel[...] = mm(perm, code, NT)
    w_rel = mm(perm, rwm.astype(BF16), NT).astype(BF16)
    mb_hot = (mb_ref[...] == iota((8, T), 0)).astype(BF16)
    cnt[0:8, :] = mm(mb_hot, picked.astype(BF16), NN)

    spread = (iota((ROWS, PER), 0) // CAP == iota((ROWS, PER), 1)).astype(BF16)
    slot_row = (iota((ROWS, T), 0) % CAP).astype(F32)
    for g in range(GROUPS):
        is_it = mm(spread, code_rel[g * PER : (g + 1) * PER, :].astype(BF16), NN) == slot_row
        weight = mm(spread, w_rel[g * PER : (g + 1) * PER, :], NN)
        hot[g * ROWS : (g + 1) * ROWS, :] = jnp.where(is_it, 1.0, 0.0).astype(BF16)
        whot[g * ROWS : (g + 1) * ROWS, :] = jnp.where(is_it, weight, 0.0).astype(BF16)

    def gather_rows(one_hot, table, out, g):
        pg[...] = mm(one_hot[rows_of(g, ROWS), :], table[...], NN).astype(BF16)
        pack(out, g)

    def pack(out, g):
        def block(n, carry):
            tile = pg[rows_of(n, BLK), :].reshape(BLK, CH, 128)
            out[rows_of(g * (ROWS // BLK) + n, BLK * CH), :] = tile.reshape(BLK * CH, 128)
            return carry

        lax.fori_loop(0, ROWS // BLK, block, 0)

    def unpack(src, g, out, out_g):
        def block(n, carry):
            tile = src[rows_of(g * (ROWS // BLK) + n, BLK * CH), :].reshape(BLK, CH, 128)
            out[rows_of(out_g * (ROWS // BLK) + n, BLK), :] = tile.reshape(BLK, D)
            return carry

        lax.fori_loop(0, ROWS // BLK, block, 0)

    def dispatch(g, carry):
        gather_rows(hot, tok_ref, sx, g)
        gather_rows(whot, cot_ref, sc, g)

        @pl.when(g == 0)
        def _():
            pl.semaphore_wait(barrier, E - 1)
            rx[0:MSG, :] = sx[0:MSG, :]
            rc[0:MSG, :] = sc[0:MSG, :]

        def send(i, carry):
            for src, dst, s_sem, r_sem in ((sx, rx, sx_sem, rx_sem), (sc, rc, sc_sem, rc_sem)):
                pltpu.make_async_remote_copy(
                    src_ref=src.at[rows_of(i, MSG)],
                    dst_ref=dst.at[rows_of(i, MSG)],
                    send_sem=s_sem,
                    recv_sem=r_sem.at[g],
                    device_id=shifted(i, 1),
                    device_id_type=MESH,
                ).start()
            return carry

        lax.fori_loop(jnp.where(g == 0, 1, g * PER), (g + 1) * PER, send, 0)
        return carry

    lax.fori_loop(0, GROUPS, dispatch, 0)

    def count_round(base, others, stage):
        copies = []
        for n in range(others):
            step = n + 1
            if stage == 0:
                to = ((x + step) % 4, ex, y)
            elif stage == 1:
                to = (x, ex, (y + step) % 4)
            else:
                to = (x, (ex + step) % 8, y)
            copies.append(
                pltpu.make_async_remote_copy(
                    src_ref=cnt.at[pl.ds(stage * 8, 8)],
                    dst_ref=cnt_in.at[pl.ds((base + n) * 8, 8)],
                    send_sem=cs_sem.at[base + n],
                    recv_sem=cr_sem.at[base + n],
                    device_id=to,
                    device_id_type=MESH,
                )
            )
        for copy in copies:
            copy.start()
        return copies

    def count_sum(copies, base, stage):
        total = cnt[stage * 8 : stage * 8 + 8, :]
        for n, copy in enumerate(copies):
            copy.wait()
            total = total + cnt_in[(base + n) * 8 : (base + n) * 8 + 8, :]
        cnt[stage * 8 + 8 : stage * 8 + 16, :] = total

    copies = count_round(0, 3, 0)
    count_sum(copies, 0, 0)
    copies = count_round(3, 3, 1)
    count_sum(copies, 3, 1)
    copies = count_round(6, 7, 2)
    for load in loads:
        load.wait()

    collect = (iota((PER, ROWS), 1) // CAP == iota((PER, ROWS), 0)).astype(BF16)
    slot_lane = (iota((ROWS, 128), 0) % CAP == iota((ROWS, 128), 1)).astype(F32)

    def expert(g, carry):
        part = rows_of(g, ROWS)

        def arrived(buf, sem):
            @pl.when(g == 0)
            def _():
                piece = buf.at[pl.ds(MSG, (PER - 1) * MSG)]
                pltpu.make_async_copy(piece, piece, sem.at[0]).wait()

            @pl.when(g > 0)
            def _():
                piece = buf.at[rows_of(g, PER * MSG)]
                pltpu.make_async_copy(piece, piece, sem.at[g]).wait()

        arrived(rx, rx_sem)
        unpack(rx, g, xs, g)
        arrived(rc, rc_sem)
        unpack(rc, g, cs, g)
        score = jnp.zeros((ROWS, 1), F32)
        for h in range(H // 256):
            cols = slice(h * 256, (h + 1) * 256)
            pre_gate = mm(xs[part, :], wg[:, cols], NN)
            pre_up = mm(xs[part, :], wu[:, cols], NN)
            back = mm(cs[part, :], wd[cols, :], NT)
            logistic = jax.nn.sigmoid(pre_gate)
            act = pre_gate * logistic
            deriv = logistic * (1.0 + pre_gate * (1.0 - logistic))
            hidden = (act * pre_up).astype(BF16)
            hid[part, cols] = hidden
            score = score + jnp.sum(hidden.astype(F32) * back, axis=1, keepdims=True)
            gu[part, cols] = (back * pre_up * deriv).astype(BF16)
            gu[part, h * 256 + H : (h + 1) * 256 + H] = (back * act).astype(BF16)
        score_rows = mm(collect, (score * slot_lane).astype(BF16), NN)
        for i in range(PER):
            qs[g * PER + i] = score_rows[i : i + 1, :]
        for n in range(4):
            cols = slice(n * 512, (n + 1) * 512)
            pair = mm(gu[part, 0:H], wg[cols, :], NT) + mm(gu[part, H : 2 * H], wu[cols, :], NT)
            pg[:, cols] = pair.astype(BF16)
        pack(ps, g)

        @pl.when(g == 0)
        def _():
            pr[0:MSG, :] = ps[0:MSG, :]
            qr[0] = qs[0]

        def send(i, carry):
            to = shifted(i, -1)
            pltpu.make_async_remote_copy(
                src_ref=ps.at[rows_of(i, MSG)],
                dst_ref=pr.at[rows_of(i, MSG)],
                send_sem=ps_sem,
                recv_sem=pr_sem.at[g],
                device_id=to,
                device_id_type=MESH,
            ).start()
            pltpu.make_async_remote_copy(
                src_ref=qs.at[pl.ds(i, 1)],
                dst_ref=qr.at[pl.ds(i, 1)],
                send_sem=qs_sem,
                recv_sem=qr_sem,
                device_id=to,
                device_id_type=MESH,
            ).start()
            return carry

        lax.fori_loop(jnp.where(g == 0, 1, g * PER), (g + 1) * PER, send, 0)
        return carry

    lax.fori_loop(0, GROUPS, expert, 0)

    def out_copies(n, slot):
        rows = rows_of(n, 256)
        return (
            pltpu.make_async_copy(out_a.at[slot, :, pl.ds(0, H)], gg_hbm.at[rows], oa_sem.at[slot, 0]),
            pltpu.make_async_copy(out_a.at[slot, :, pl.ds(H, H)], gu_hbm.at[rows], oa_sem.at[slot, 1]),
        )

    def grad_in(n, carry):
        slot = n % 2

        @pl.when(n >= 2)
        def _():
            for copy in out_copies(n - 2, slot):
                copy.wait()

        out_a[slot] = mm(xs[:, rows_of(n, 256)], gu[...], TN).astype(BF16)
        for copy in out_copies(n, slot):
            copy.start()
        return carry

    lax.fori_loop(0, D // 256, grad_in, 0)

    def down_copy(n, slot):
        return pltpu.make_async_copy(out_d.at[slot], gd_hbm.at[rows_of(n, 256)], od_sem.at[slot])

    def grad_out(n, carry):
        slot = n % 2

        @pl.when(n >= 2)
        def _():
            down_copy(n - 2, slot).wait()

        out_d[slot] = mm(hid[:, rows_of(n, 256)], cs[...], TN).astype(BF16)
        down_copy(n, slot).start()
        return carry

    lax.fori_loop(0, H // 256, grad_out, 0)

    count_sum(copies, 6, 2)
    load = cnt[24:32, :] * (E * MICRO / (K * T * E))
    batch_col = jnp.transpose((mb_ref[...] == iota((T, T), 0)).astype(F32))[:, 1:2]
    token_load = jnp.where(batch_col > 0.0, load[1:2, :], load[0:1, :])
    prob = prob_ref[...]
    gb_ref[...] = prob * (token_load - jnp.sum(prob * token_load, axis=1, keepdims=True))

    acc[...] = jnp.zeros_like(acc)

    def combine(g, carry):
        @pl.when(g == 0)
        def _():
            piece = pr.at[pl.ds(MSG, (PER - 1) * MSG)]
            pltpu.make_async_copy(piece, piece, pr_sem.at[0]).wait()

        @pl.when(g > 0)
        def _():
            piece = pr.at[rows_of(g, PER * MSG)]
            pltpu.make_async_copy(piece, piece, pr_sem.at[g]).wait()

        unpack(pr, g, pg, 0)
        acc[...] += mm(hot[rows_of(g, ROWS), :], pg[...], TN)
        return carry

    lax.fori_loop(0, GROUPS, combine, 0)
    gt_ref[...] = acc[...].astype(BF16)

    pltpu.make_async_copy(qr.at[pl.ds(1, E - 1)], qr.at[pl.ds(1, E - 1)], qr_sem).wait()
    q_all = jnp.concatenate([qr[i] for i in range(E)], axis=0)
    q_rel = jnp.zeros((E, T), F32)
    for s in range(CAP):
        q_rel = jnp.where(code_rel[...] == float(s), q_all[:, s : s + 1], q_rel)
    q = mm(q_rel.astype(BF16), perm_ref[...], TN)
    gl_ref[...] = q - rwm_ref[...] * jnp.sum(q, axis=1, keepdims=True)

    for n in (D // 256 - 2, D // 256 - 1):
        for copy in out_copies(n, n % 2):
            copy.wait()
    for n in (H // 256 - 2, H // 256 - 1):
        down_copy(n, n % 2).wait()
    for buf, sem in ((sx, sx_sem), (sc, sc_sem), (ps, ps_sem)):
        piece = buf.at[pl.ds(MSG, (E - 1) * MSG)]
        pltpu.make_async_copy(piece, piece, sem).wait()
    pltpu.make_async_copy(qs.at[pl.ds(1, E - 1)], qs.at[pl.ds(1, E - 1)], qs_sem).wait()


def per_device(tokens, out_grad, router_logits, expert_picks, micro_batch, w_gate, w_up, w_down):
    vmem, hbm = pl.BlockSpec(memory_space=pltpu.VMEM), pl.BlockSpec(memory_space=pl.ANY)
    dma = pltpu.SemaphoreType.DMA
    outs = pl.pallas_call(
        kernel,
        out_shape=(
            jax.ShapeDtypeStruct((T, D), BF16),
            jax.ShapeDtypeStruct((T, E), F32),
            jax.ShapeDtypeStruct((T, E), F32),
            jax.ShapeDtypeStruct((D, H), BF16),
            jax.ShapeDtypeStruct((D, H), BF16),
            jax.ShapeDtypeStruct((H, D), BF16),
        ),
        in_specs=[vmem] * 5 + [hbm] * 3,
        out_specs=(vmem,) * 3 + (hbm,) * 3,
        scratch_shapes=[
            *[pltpu.VMEM((E * MSG, 128), BF16)] * 6,
            *[pltpu.VMEM((PAIRS, D), BF16)] * 2,
            pltpu.VMEM((PAIRS, H), BF16),
            pltpu.VMEM((PAIRS, 2 * H), BF16),
            pltpu.VMEM((D, H), BF16),
            pltpu.VMEM((D, H), BF16),
            pltpu.VMEM((H, D), BF16),
            pltpu.VMEM((ROWS, D), BF16),
            pltpu.VMEM((PAIRS, T), BF16),
            pltpu.VMEM((PAIRS, T), BF16),
            pltpu.VMEM((E, T), F32),
            pltpu.VMEM((E, E), BF16),
            pltpu.VMEM((T, E), F32),
            pltpu.VMEM((T, E), F32),
            pltpu.VMEM((E, 1, 128), F32),
            pltpu.VMEM((E, 1, 128), F32),
            pltpu.VMEM((T, D), F32),
            pltpu.VMEM((32, E), F32),
            pltpu.VMEM((13 * 8, E), F32),
            pltpu.VMEM((2, 256, 2 * H), BF16),
            pltpu.VMEM((2, 256, D), BF16),
            dma((3,)), dma, dma, dma((GROUPS,)), dma((GROUPS,)), dma, dma((GROUPS,)), dma, dma,
            dma((13,)), dma((13,)), dma((2, 2)), dma((2,)),
        ],
        compiler_params=pltpu.CompilerParams(
            collective_id=0, has_side_effects=True, vmem_limit_bytes=64 * 2**20
        ),
        name="expert_backward",
    )(tokens, out_grad, router_logits, expert_picks, micro_batch.reshape(1, T), w_gate[0], w_up[0], w_down[0])
    grad_tokens, grad_logits, balance_grad, grad_gate, grad_up, grad_down = outs
    return grad_tokens, grad_logits, balance_grad, grad_gate[None], grad_up[None], grad_down[None]


def solution(mesh):
    rows, cube = P(("dp", "ex", "ey"), None), P(("dp", "ex", "ey"), None, None)
    return jax.shard_map(
        per_device,
        mesh=mesh,
        in_specs=(rows, rows, rows, rows, P(("dp", "ex", "ey")), cube, cube, cube),
        out_specs=(rows, rows, rows, cube, cube, cube),
        check_vma=False,
    )
```

time: 593 us -> 220 us (0.37); the launches traced: 585 us -> 220 us
  blocking collectives: 280 us -> 0 us
  Pallas kernels: 0 us -> 204 us
  local copies, waits for them, and re-layouts: 116 us -> 14.8 us
  waiting for transfers between devices: 83.1 us -> 0 us
  matrix products: 60.1 us -> 0 us
  other arithmetic: 25.4 us -> 0 us
  starting transfers between devices: 19 us -> 0 us
    pallas_call x0 -> x1, Pallas kernels: none -> 204 us  [per_device(): pl.pallas_call(kernel, out_shape=(jax.ShapeDtypeStruct((T, D), BF16), jax...]
    psum x1 -> x0, blocking collectives: 156 us -> none  [per_device(): occupancy = lax.psum(part_counts, ('dp', 'ex', 'ey'))]
    all_to_all x2 -> x0, blocking collectives: 124 us -> none  [the longest x1 110 us: per_device(): lax.all_to_all(token_send, ('dp', 'ex', 'ey'), split_axis=0, concat_axis=...]
    all_to_all x3 -> x0, waiting for transfers between devices: 83.1 us -> none  [the longest x1 73.3 us: per_device(): lax.all_to_all(cotangent_send, ('dp', 'ex', 'ey'), split_axis=0, concat_a...]
    gather x12 -> x0, local copies, waits for them, and re-layouts: 72.9 us -> none  [the longest x2 19.8 us: per_device(): token_send = jnp.where(occupied[:, None], tokens[source_token], 0)]
    dot_general x9 -> x0, matrix products: 60.1 us -> none  [the longest x1 12.2 us: expert_backward(): lax.dot_general(cotangent_rows, down_matrix, contract_cols, preferred_ele...]
    reshape x5 -> x0, local copies, waits for them, and re-layouts: 33.9 us -> none  [the longest x1 8.68 us: per_device(): cotangent_recv.reshape(experts * capacity, model_width)]
    all_to_all x3 -> x0, starting transfers between devices: 19 us -> none  [the longest x1 7.53 us: per_device(): lax.all_to_all(cotangent_send, ('dp', 'ex', 'ey'), split_axis=0, concat_a...]
  transfers between devices with their start and end apart: 3 -> 0, of which waited for: 2 -> 0; matrix products, arithmetic and copies ran while one was open for 10% -> 0% of each run, Pallas kernels for 0% -> 0%
where the time goes in v1:
time: 220 us
  Pallas kernels  204 us (93%)
  local copies, waits for them, and re-layouts  14.8 us (7%)
    pallas_call x1, Pallas kernels, per_device(): pl.pallas_call(kernel, out_shape=(jax.ShapeDtypeStruct((T, D), BF16), jax...  204 us
    unnamed x11, local copies, waits for them, and re-layouts  14.8 us

profile of v1, /device:TPU:1, one launch (start us, length us, event | category | flops | bytes accessed | tf_op | source)
XLA Modules:
  0.0 219.8 jit_solution(18225660248596421872)
XLA Ops:
  0.6 1.4 copy.14.pick_ref
  2.0 204.4 %expert_backward.1 = (bf16[128,2048]{1,0:T(8,128)(2,1)}, f32[128,128]{1,0:T(8,128)}, f32[128,128]{1,0:T(8,128)}, bf16[2048,768]{1,0:T(8,128)(2,1)}, bf16[2048,76...) custom-call(bf16[128,2048]{1,0:T(8,128)(2,1)} %tok_ref.1, bf16[128,2048]{1,0:T(8,128)(2,1)} %cot_ref.1, f32[128,128]{1,0:T(8,128)} %logit_ref.1, ...), custom_call_target="tpu_custom_call" | custom-call | tf_op jit(solution)/shard_map/expert_backward/pallas_call | solution.py:359
  206.4 1.9 copy.21
  208.3 1.5 copy.22
  209.8 1.5 copy.23
  211.2 0.0 copy-start.1
  211.2 3.9 %copy.24 = bf16[1,2048,768]{2,1,0:T(8,128)(2,1)} copy(bf16[1,2048,768]{2,1,0:T(8,128)(2,1)} %bitcast.9) | data formatting | bytes 6291456
  215.1 0.0 copy-done.1
  215.2 0.0 copy-start
  215.2 1.7 copy.25
  216.8 1.4 copy-done
  218.2 1.7 copy.26
Async XLA Ops:
  211.2 3.9 %copy-start.1 = (bf16[2048,768]{1,0:T(8,128)(2,1)S(1)}, bf16[2048,768]{1,0:T(8,128)(2,1)}, u32[]{:S(2)}) copy-start(bf16[2048,768]{1,0:T(8,128)(2,1)} %get-tuple-element.16) | copy-start | bytes 9437188
  215.2 3.0 %copy-start = (bf16[768,2048]{1,0:T(8,128)(2,1)S(1)}, bf16[768,2048]{1,0:T(8,128)(2,1)}, u32[]{:S(2)}) copy-start(bf16[768,2048]{1,0:T(8,128)(2,1)} %get-tuple-element.17) | copy-start | bytes 9437188

commit v2 on v1

v2 whole, which is shorter than its diff:
```python
import jax
import jax.numpy as jnp
from jax import lax
from jax.experimental import pallas as pl
from jax.experimental.pallas import tpu as pltpu
from jax.sharding import PartitionSpec as P

MESH = pl.DeviceIdType.MESH
F32, BF16, I32 = jnp.float32, jnp.bfloat16, jnp.int32
NN = (((1,), (0,)), ((), ()))
NT = (((1,), (1,)), ((), ()))
TN = (((0,), (0,)), ((), ()))

D, H, K, T, E, CAP, MICRO = 2048, 768, 8, 128, 128, 9, 2
AXES = 3
LINE = 4
PLANE = E // LINE
GROUPS = 2
PER = PLANE // GROUPS
MSG = LINE * CAP
ROWS = PER * MSG
PAIRS = E * CAP
HALF = ROWS // 2
SHEET = LINE * MSG
BLK = 32
Q_TOK, Q_COT, Q_PAIR = (4, 4, 8), (4, 8, 4), (8, 4, 4)


def slices(chunks):
    starts = [sum(chunks[:a]) * 128 for a in range(AXES)]
    return [slice(s, s + q * 128) for s, q in zip(starts, chunks)]


COLS_TOK, COLS_COT, COLS_PAIR = slices(Q_TOK), slices(Q_COT), slices(Q_PAIR)
PAIR_HOME = (2, 1, 0)


def mm(a, b, dims):
    return lax.dot_general(a, b, dims, preferred_element_type=F32)


def rows_of(g, size):
    return pl.ds(pl.multiple_of(g * size, size), size)


def iota(shape, dim):
    return lax.broadcasted_iota(I32, shape, dim)


def moved(dx, dy, dz, dc, sign=1):
    x, ex, y = lax.axis_index("dp"), lax.axis_index("ex"), lax.axis_index("ey")
    return (
        (x + sign * dx + 4) % 4,
        (ex // 2 + sign * dz + 4) % 4 * 2 + (ex % 2 + dc) % 2,
        (y + sign * dy + 4) % 4,
    )


def along(axis, step, sign=1):
    return moved(*(step if axis == n else 0 for n in range(AXES)), 0, sign)


def in_plane(axis, j, sign=1):
    core, high, low = j // 16, (j // 4) % 4, j % 4
    place = ((0, low, high), (low, 0, high), (low, high, 0))[axis]
    return moved(*place, core, sign)


def any_offset(i, sign=1):
    return moved(i % 4, (i // 4) % 4, (i // 16) % 4, i // 64, sign)


def turn(n):
    return (n % 4 + n // 4) % 4 * 4 + n % 4


def expert_at(dx, dy, dz, dc):
    x, ex, y = lax.axis_index("dp"), lax.axis_index("ex"), lax.axis_index("ey")
    return ((x + dx) & 3) * 32 + ((((ex // 2) + dz) & 3) * 2 + (((ex % 2) + dc) & 1)) * 4 + ((y + dy) & 3)


def kernel(
    tok_hbm, cot_hbm, logit_ref, pick_ref, mb_ref, wg_hbm, wu_hbm, wd_hbm,
    gt_ref, gl_ref, gb_ref, gg_hbm, gu_hbm, gd_hbm,
    st0, st1, st2, sc0, sc1, sc2, rt0, rt1, rt2, rc0, rc1, rc2, pr0, pr1, pr2,
    tt0, tt1, tt2, tc0, tc1, tc2, hot0, hot1, hot2, fr0, fr1, fr2, perm_y, perm_z,
    xs, cs, hid, gu, wg, wu, wd, pg, out_buf, cw, cwg, code_rel, perm_ref, rwm_ref, qs, qr, cnt, cnt_in,
    w_sem, own_sem, gt_s, gt_r, gc_s, gc_r, gw_s, gw_r, st_sem, sc_sem, rt_sem, rc_sem, ps_sem, pr_sem, fs_sem, fr_sem,
    qs_sem, qr_sem, cs_sem, cr_sem, oa_sem, od_sem,
):
    x, ex, y = lax.axis_index("dp"), lax.axis_index("ex"), lax.axis_index("ey")
    st, sc, rt, rc, pr = (st0, st1, st2), (sc0, sc1, sc2), (rt0, rt1, rt2), (rc0, rc1, rc2), (pr0, pr1, pr2)
    tt, tc, hot, fr = (tt0, tt1, tt2), (tc0, tc1, tc2), (hot0, hot1, hot2), (fr0, fr1, fr2)
    ps = tuple(st[n] for n in PAIR_HOME)
    fs = tuple(tt[n] for n in PAIR_HOME)
    barrier = pltpu.get_barrier_semaphore()

    def greet(i, carry):
        pl.semaphore_signal(barrier, inc=1, device_id=any_offset(i), device_id_type=MESH)
        return carry

    lax.fori_loop(1, E, greet, 0)
    loads = [
        pltpu.make_async_copy(src, dst, w_sem.at[n])
        for n, (src, dst) in enumerate(((wg_hbm, wg), (wu_hbm, wu), (wd_hbm, wd)))
    ]
    own = []
    for a in range(AXES):
        own.append(pltpu.make_async_copy(tok_hbm.at[:, COLS_TOK[a]], tt[a].at[pl.ds(0, T)], own_sem.at[0, a]))
        own.append(pltpu.make_async_copy(cot_hbm.at[:, COLS_COT[a]], tc[a].at[pl.ds(0, T)], own_sem.at[1, a]))
    for load in own + loads:
        load.start()

    def remote(src, dst, send_sem, recv_sem, to):
        pltpu.make_async_remote_copy(
            src_ref=src, dst_ref=dst, send_sem=send_sem, recv_sem=recv_sem, device_id=to, device_id_type=MESH
        ).start()

    def await_bytes(piece, sem):
        pltpu.make_async_copy(piece, piece, sem).wait()

    expert_row = iota((E, T), 0)
    picked_t = jnp.zeros((E, T), F32)
    for k in range(K):
        picked_t = jnp.where(pick_ref[k : k + 1, :] == expert_row, 1.0, picked_t)
    picked = jnp.transpose(picked_t)
    logits = logit_ref[...]
    top = jnp.max(jnp.where(picked > 0.0, logits, -jnp.inf), axis=1, keepdims=True)
    rwm = jnp.where(picked > 0.0, jnp.exp(jnp.minimum(logits - top, 0.0)), 0.0)
    rwm = rwm / jnp.sum(rwm, axis=1, keepdims=True)
    rwm_ref[...] = rwm
    weight = rwm.astype(BF16)
    earlier = (iota((T, T), 1) < iota((T, T), 0)).astype(BF16)
    code = jnp.where(picked > 0.0, mm(earlier, picked.astype(BF16), NN) + 1.0, 0.0).astype(BF16)
    row, lane = iota((E, E), 0), iota((E, E), 1)
    perm = (expert_at(row & 3, (row >> 2) & 3, (row >> 4) & 3, row >> 6) == lane).astype(BF16)
    perm_ref[...] = perm
    code_rel[...] = mm(perm, code, NT)
    step, core, high, low = row >> 5, (row >> 4) & 1, (row >> 2) & 3, row & 3
    for a in range(AXES):
        place = ((step, low, high), (low, step, high), (low, high, step))[a]
        perm = (expert_at(*place, core) == lane).astype(BF16)
        code_a, weight_a = mm(perm, code, NT).astype(BF16), mm(perm, weight, NT).astype(BF16)
        for s in range(LINE):
            home = cw if s else cwg
            home[a, s * 64 : s * 64 + 32, :] = code_a[s * 32 : s * 32 + 32, :]
            home[a, s * 64 + 32 : s * 64 + 64, :] = weight_a[s * 32 : s * 32 + 32, :]
    mb_hot = (mb_ref[...] == iota((8, T), 0)).astype(BF16)
    cnt[0:8, :] = mm(mb_hot, picked.astype(BF16), NN)
    pl.semaphore_wait(barrier, E - 1)

    for s in (1, 3, 2):
        for a in range(AXES):
            home = tt[a].at[pl.ds(s * T, T)]
            remote(tok_hbm.at[:, COLS_TOK[a]], home, gt_s.at[a], gt_r.at[a], along(a, s))
    for s in (1, 3, 2):
        for a in range(AXES):
            piece = pl.ds(s * 64, 64)
            remote(cw.at[a, piece], cwg.at[a, piece], gw_s.at[a], gw_r.at[a], along(a, s))
    for s in (1, 3, 2):
        for a in range(AXES):
            home = tc[a].at[pl.ds(s * T, T)]
            remote(cot_hbm.at[:, COLS_COT[a]], home, gc_s.at[a], gc_r.at[a], along(a, s))

    def count_round(base, others, stage):
        copies = []
        for n in range(others):
            to = (
                ((x + n + 1) % 4, ex, y),
                (x, ex, (y + n + 1) % 4),
                (x, (ex + n + 1) % 8, y),
            )[stage]
            copies.append(
                pltpu.make_async_remote_copy(
                    src_ref=cnt.at[pl.ds(stage * 8, 8)],
                    dst_ref=cnt_in.at[pl.ds((base + n) * 8, 8)],
                    send_sem=cs_sem.at[base + n],
                    recv_sem=cr_sem.at[base + n],
                    device_id=to,
                    device_id_type=MESH,
                )
            )
        for copy in copies:
            copy.start()
        return copies

    def count_sum(copies, base, stage):
        total = cnt[stage * 8 : stage * 8 + 8, :]
        for n, copy in enumerate(copies):
            copy.wait()
            total = total + cnt_in[(base + n) * 8 : (base + n) * 8 + 8, :]
        cnt[stage * 8 + 8 : stage * 8 + 16, :] = total

    copies = count_round(0, 3, 0)


    def order_block(n, carry):
        pair = iota((64, 1), 0) + n * 64
        s_, x_, y_, z_ = pair % CAP, pair // 9 % 4, pair // 36 % 4, pair // 144
        perm_z[rows_of(n, 64), :] = (((y_ * 4 + x_) * 4 + z_) * CAP + s_ == iota((64, ROWS), 1)).astype(BF16)
        return carry

    lax.fori_loop(0, ROWS // 64, order_block, 0)
    pair = iota((SHEET, 1), 0)
    perm_y[...] = ((pair // 9 % 4 * 4 + pair // 36) * CAP + pair % CAP == iota((SHEET, SHEET), 1)).astype(BF16)
    for load in own:
        load.wait()

    def pack(out, g, q):
        def block(n, carry):
            tile = pg[rows_of(n, BLK), 0 : q * 128].reshape(BLK, q, 128)
            out[rows_of(g * (ROWS // BLK) + n, BLK * q), :] = tile.reshape(BLK * q, 128)
            return carry

        lax.fori_loop(0, ROWS // BLK, block, 0)

    def unpack(src, g, q, out, out_g):
        def block(n, carry):
            tile = src[rows_of(g * (ROWS // BLK) + n, BLK * q), :].reshape(BLK, q, 128)
            out[rows_of(out_g * (ROWS // BLK) + n, BLK), 0 : q * 128] = tile.reshape(BLK, q * 128)
            return carry

        lax.fori_loop(0, ROWS // BLK, block, 0)

    def own_message(g, src, dst, q):
        @pl.when(g == 0)
        def _():
            dst[0 : MSG * q, :] = src[0 : MSG * q, :]

    def send_group(g, parts, sign):
        def send(n, carry):
            j = g * PER + turn(n)
            for a, (src, dst, s_sem, r_sem, q) in enumerate(parts):
                piece = rows_of(j, MSG * q)
                remote(src.at[piece], dst.at[piece], s_sem.at[g, a], r_sem.at[g, a], in_plane(a, j, sign))
            return carry

        lax.fori_loop(jnp.where(g == 0, 1, 0), PER, send, 0)

    def await_group(g, buf, sem, a, q):
        @pl.when(g == 0)
        def _():
            await_bytes(buf.at[pl.ds(MSG * q, (PER - 1) * MSG * q)], sem.at[0, a])

        @pl.when(g > 0)
        def _():
            await_bytes(buf.at[rows_of(g, ROWS * q)], sem.at[g, a])

    slot = (iota((ROWS, T), 0) % CAP + 1).astype(F32)

    def pick_rows(a, g, s):
        pair, j = iota((ROWS, PER), 0), iota((ROWS, PER), 1)
        return jnp.logical_and(pair // MSG == j, pair // CAP % LINE == s).astype(BF16)

    def fill(one_hot, table, q):
        def half(n, carry):
            for c in range(0, q, 4):
                lanes = slice(c * 128, (c + 4) * 128)
                pg[rows_of(n, HALF), lanes] = mm(one_hot(n), table[:, lanes], NN).astype(BF16)
            return carry

        lax.fori_loop(0, 2, half, 0)

    def dispatch(g, carry):
        part = rows_of(g, ROWS)
        for a in range(AXES):

            @pl.when(g == 0)
            def _():
                await_bytes(cwg.at[a, pl.ds(64, 192)], gw_r.at[a])

            for s in range(LINE):
                found = mm(pick_rows(a, g, s), cwg[a, pl.ds(s * 64 + g * PER, PER), :], NN)
                hot[a][part, s * T : (s + 1) * T] = (found == slot).astype(BF16)
        for a in range(AXES):

            @pl.when(g == 0)
            def _():
                await_bytes(tt[a].at[pl.ds(T, 3 * T)], gt_r.at[a])

            fill(lambda rows: hot[a][rows_of(2 * g + rows, HALF), :], tt[a], Q_TOK[a])
            pack(st[a], g, Q_TOK[a])
            own_message(g, st[a], rt[a], Q_TOK[a])
        send_group(g, [(st[a], rt[a], st_sem, rt_sem, Q_TOK[a]) for a in range(AXES)], 1)
        for a in range(AXES):
            for s in range(LINE):
                lanes = slice(s * T, (s + 1) * T)
                scale = mm(pick_rows(a, g, s), cwg[a, pl.ds(s * 64 + 32 + g * PER, PER), :], NN)
                xs[0:ROWS, lanes] = (hot[a][part, lanes].astype(F32) * scale).astype(BF16)

            @pl.when(g == 0)
            def _():
                await_bytes(tc[a].at[pl.ds(T, 3 * T)], gc_r.at[a])

            fill(lambda rows: xs[rows_of(rows, HALF), 0 : LINE * T], tc[a], Q_COT[a])
            pack(sc[a], g, Q_COT[a])
            own_message(g, sc[a], rc[a], Q_COT[a])
        send_group(g, [(sc[a], rc[a], sc_sem, rc_sem, Q_COT[a]) for a in range(AXES)], 1)
        return carry

    lax.fori_loop(0, GROUPS, dispatch, 0)
    count_sum(copies, 0, 0)
    copies = count_round(3, 3, 1)
    for load in loads:
        load.wait()

    def reorder(a, src, src_col, dst, dst_rows, dst_col, q, dims):
        for c in range(0, q * 128, 256):
            rows, lanes = src(slice(src_col + c, src_col + c + 256)), slice(dst_col + c, dst_col + c + 256)
            if a == 1:
                sheets = [rows[n * SHEET : (n + 1) * SHEET, :] for n in range(ROWS // SHEET)]
                rows = jnp.concatenate([mm(perm_y[...], sheet, dims).astype(BF16) for sheet in sheets], axis=0)
            elif a == 2:
                rows = mm(perm_z[...], rows, dims).astype(BF16)
            dst[dst_rows, lanes] = rows

    collect = (iota((2 * PER, HALF), 1) // CAP == iota((2 * PER, HALF), 0)).astype(BF16)
    slot_lane = (iota((HALF, 128), 0) % CAP == iota((HALF, 128), 1)).astype(F32)

    def expert(g, carry):
        part = rows_of(g, ROWS)
        for out, src, sem, chunks, cols in ((xs, rt, rt_sem, Q_TOK, COLS_TOK), (cs, rc, rc_sem, Q_COT, COLS_COT)):
            for a in range(AXES):
                await_group(g, src[a], sem, a, chunks[a])
                unpack(src[a], g, chunks[a], pg, 0)
                reorder(a, lambda lanes: pg[:, lanes], 0, out, part, cols[a].start, chunks[a], NN)

        def hidden_rows(n, carry):
            part = rows_of(2 * g + n, HALF)
            score = jnp.zeros((HALF, 1), F32)
            for h in range(H // 256):
                cols = slice(h * 256, (h + 1) * 256)
                pre_gate = mm(xs[part, :], wg[:, cols], NN)
                pre_up = mm(xs[part, :], wu[:, cols], NN)
                back = mm(cs[part, :], wd[cols, :], NT)
                logistic = jax.nn.sigmoid(pre_gate)
                act = pre_gate * logistic
                deriv = logistic * (1.0 + pre_gate * (1.0 - logistic))
                hidden = (act * pre_up).astype(BF16)
                hid[part, cols] = hidden
                score = score + jnp.sum(hidden.astype(F32) * back, axis=1, keepdims=True)
                gu[part, cols] = (back * pre_up * deriv).astype(BF16)
                gu[part, h * 256 + H : (h + 1) * 256 + H] = (back * act).astype(BF16)
            score_rows = mm(collect, (score * slot_lane).astype(BF16), NN)
            for i in range(2 * PER):
                qs[(2 * g + n) * 2 * PER + i] = score_rows[i : i + 1, :]
            return carry

        lax.fori_loop(0, 2, hidden_rows, 0)
        for a in range(AXES):
            q, first = Q_PAIR[a], COLS_PAIR[a].start

            def pair_cols(lanes):
                rows = mm(gu[part, 0:H], wg[lanes, :], NT) + mm(gu[part, H : 2 * H], wu[lanes, :], NT)
                return rows.astype(BF16)

            reorder(a, pair_cols, first, pg, slice(0, ROWS), 0, q, TN)
            await_group(g, st[PAIR_HOME[a]], st_sem, PAIR_HOME[a], q)
            pack(ps[a], g, q)
            own_message(g, ps[a], pr[a], q)
        send_group(g, [(ps[a], pr[a], ps_sem, pr_sem, Q_PAIR[a]) for a in range(AXES)], -1)
        @pl.when(g == 0)
        def _():
            qr[0] = qs[0]

        def send_score(i, carry):
            remote(qs.at[pl.ds(i, 1)], qr.at[pl.ds(i, 1)], qs_sem, qr_sem, any_offset(i, -1))
            return carry

        lax.fori_loop(jnp.where(g == 0, 1, g * 4 * PER), (g + 1) * 4 * PER, send_score, 0)
        return carry

    lax.fori_loop(0, GROUPS, expert, 0)
    count_sum(copies, 3, 1)
    copies = count_round(6, 7, 2)

    def in_copies(n, buf):
        rows = rows_of(n, 256)
        return (
            pltpu.make_async_copy(out_buf.at[buf, :, pl.ds(0, H)], gg_hbm.at[rows], oa_sem.at[buf, 0]),
            pltpu.make_async_copy(out_buf.at[buf, :, pl.ds(H, H)], gu_hbm.at[rows], oa_sem.at[buf, 1]),
        )

    def grad_in(n, carry):
        buf = n % 2

        @pl.when(n >= 2)
        def _():
            for copy in in_copies(n - 2, buf):
                copy.wait()

        turned = jnp.transpose(xs[:, rows_of(n, 256)])
        for part in (slice(0, H), slice(H, 2 * H)):
            out_buf[buf, :, part] = mm(turned, gu[:, part], NN).astype(BF16)
        for copy in in_copies(n, buf):
            copy.start()
        return carry

    lax.fori_loop(0, D // 256, grad_in, 0)
    for n in (D // 256 - 2, D // 256 - 1):
        for copy in in_copies(n, n % 2):
            copy.wait()

    for a in range(AXES):
        q = Q_PAIR[a]
        for g in range(GROUPS):
            await_group(g, pr[a], pr_sem, a, q)
            unpack(pr[a], g, q, xs, g)
        for c in range(0, q, 4):
            lanes = slice(c * 128, (c + 4) * 128)
            fs[a][:, lanes] = mm(hot[a][...], xs[:, lanes], TN).astype(BF16)
        for s in (1, 3, 2):
            piece = fr[a].at[pl.ds((s - 1) * T, T)]
            remote(fs[a].at[pl.ds(s * T, T)], piece, fs_sem.at[a], fr_sem.at[a], along(a, s, -1))

    def down_copy(n, buf):
        place = gd_hbm.at[rows_of(n // 2, 256), rows_of(n % 2, D // 2)]
        return pltpu.make_async_copy(out_buf.at[buf, :, pl.ds(0, D // 2)], place, od_sem.at[buf])

    def grad_out(n, carry):
        buf = n % 2

        @pl.when(n >= 2)
        def _():
            down_copy(n - 2, buf).wait()

        rows = mm(hid[:, rows_of(n // 2, 256)], cs[:, rows_of(n % 2, D // 2)], TN)
        out_buf[buf, :, 0 : D // 2] = rows.astype(BF16)
        down_copy(n, buf).start()
        return carry

    lax.fori_loop(0, H // 128, grad_out, 0)

    prob = jnp.exp(logit_ref[...] - jnp.max(logit_ref[...], axis=1, keepdims=True))
    prob = prob / jnp.sum(prob, axis=1, keepdims=True)
    count_sum(copies, 6, 2)
    load = cnt[24:32, :] * (E * MICRO / (K * T * E))
    batch_col = jnp.transpose((mb_ref[...] == iota((T, T), 0)).astype(F32))[:, 1:2]
    token_load = jnp.where(batch_col > 0.0, load[1:2, :], load[0:1, :])
    gb_ref[...] = prob * (token_load - jnp.sum(prob * token_load, axis=1, keepdims=True))

    await_bytes(qr.at[pl.ds(1, E - 1)], qr_sem)
    q_all = jnp.concatenate([qr[i] for i in range(E)], axis=0)
    q_rel = jnp.zeros((E, T), F32)
    for s in range(CAP):
        q_rel = jnp.where(code_rel[...] == float(s + 1), q_all[:, s : s + 1], q_rel)
    q_own = mm(q_rel.astype(BF16), perm_ref[...], TN)
    gl_ref[...] = q_own - rwm_ref[...] * jnp.sum(q_own, axis=1, keepdims=True)

    for a in range(AXES):
        await_bytes(fr[a], fr_sem.at[a])
        total = fs[a][0:T, :].astype(F32)
        for s in range(LINE - 1):
            total = total + fr[a][s * T : (s + 1) * T, :].astype(F32)
        gt_ref[:, COLS_PAIR[a]] = total.astype(BF16)

    for n in (H // 128 - 2, H // 128 - 1):
        down_copy(n, n % 2).wait()
    for a in range(AXES):
        await_bytes(tt[a].at[pl.ds(T, 3 * T)], gt_s.at[a])
        await_bytes(tc[a].at[pl.ds(T, 3 * T)], gc_s.at[a])
        await_bytes(cw.at[a, pl.ds(64, 192)], gw_s.at[a])
        await_bytes(fr[a], fs_sem.at[a])
        for g in range(GROUPS):
            await_group(g, sc[a], sc_sem, a, Q_COT[a])
            await_group(g, ps[a], ps_sem, a, Q_PAIR[a])
    await_bytes(qs.at[pl.ds(1, E - 1)], qs_sem)


def settle_kernel(*refs):
    sources, targets, sem, held = refs[:6], refs[6:12], refs[12], refs[13:]
    copies = []
    for src, dst, buf in zip(sources, targets, held):
        pieces = 8 if src.shape[0] > T else 1
        size = src.shape[0] // pieces
        for n in range(pieces):
            rows = pl.ds(n * size, size)
            m = len(copies)
            copies.append(
                (
                    pltpu.make_async_copy(src.at[rows], buf.at[rows], sem.at[0, m]),
                    pltpu.make_async_copy(buf.at[rows], dst.at[rows], sem.at[1, m]),
                )
            )
    for fetch, _ in copies:
        fetch.start()
    for fetch, store in copies:
        fetch.wait()
        store.start()
    for _, store in copies:
        store.wait()


def settle(outs):
    hbm = pl.BlockSpec(memory_space=pl.ANY)
    return pl.pallas_call(
        settle_kernel,
        out_shape=tuple(jax.ShapeDtypeStruct(o.shape, o.dtype) for o in outs),
        in_specs=[hbm] * 6,
        out_specs=(hbm,) * 6,
        scratch_shapes=[pltpu.SemaphoreType.DMA((2, 27))] + [pltpu.VMEM(o.shape, o.dtype) for o in outs],
        compiler_params=pltpu.CompilerParams(vmem_limit_bytes=60 * 2**20),
        name="settle",
    )(*outs)


def per_device(tokens, out_grad, router_logits, expert_picks, micro_batch, w_gate, w_up, w_down):
    vmem, hbm = pl.BlockSpec(memory_space=pltpu.VMEM), pl.BlockSpec(memory_space=pl.ANY)
    dma = pltpu.SemaphoreType.DMA

    def sliced(rows, chunks):
        return [pltpu.VMEM((rows * q, 128), BF16) for q in chunks]

    outs = pl.pallas_call(
        kernel,
        out_shape=(
            jax.ShapeDtypeStruct((T, D), BF16),
            jax.ShapeDtypeStruct((T, E), F32),
            jax.ShapeDtypeStruct((T, E), F32),
            jax.ShapeDtypeStruct((D, H), BF16),
            jax.ShapeDtypeStruct((D, H), BF16),
            jax.ShapeDtypeStruct((H, D), BF16),
        ),
        in_specs=[hbm] * 2 + [vmem] * 3 + [hbm] * 3,
        out_specs=(vmem,) * 3 + (hbm,) * 3,
        scratch_shapes=[
            *sliced(PAIRS, Q_TOK), *sliced(PAIRS, Q_COT),
            *sliced(PAIRS, Q_TOK), *sliced(PAIRS, Q_COT), *sliced(PAIRS, Q_PAIR),
            *[pltpu.VMEM((LINE * T, q * 128), BF16) for q in Q_TOK],
            *[pltpu.VMEM((LINE * T, q * 128), BF16) for q in Q_COT],
            *[pltpu.VMEM((PAIRS, LINE * T), BF16)] * AXES,
            *[pltpu.VMEM((3 * T, q * 128), BF16) for q in Q_PAIR],
            pltpu.VMEM((SHEET, SHEET), BF16), pltpu.VMEM((ROWS, ROWS), BF16),
            *[pltpu.VMEM((PAIRS, D), BF16)] * 2,
            pltpu.VMEM((PAIRS, H), BF16),
            pltpu.VMEM((PAIRS, 2 * H), BF16),
            pltpu.VMEM((D, H), BF16),
            pltpu.VMEM((D, H), BF16),
            pltpu.VMEM((H, D), BF16),
            pltpu.VMEM((ROWS, 1024), BF16),
            pltpu.VMEM((2, 256, 2 * H), BF16),
            pltpu.VMEM((AXES, 256, T), BF16),
            pltpu.VMEM((AXES, 256, T), BF16),
            pltpu.VMEM((E, T), F32),
            pltpu.VMEM((E, E), BF16),
            pltpu.VMEM((T, E), F32),
            pltpu.VMEM((E, 1, 128), F32),
            pltpu.VMEM((E, 1, 128), F32),
            pltpu.VMEM((32, E), F32),
            pltpu.VMEM((13 * 8, E), F32),
            dma((3,)),
            dma((2, AXES)),
            *[dma((AXES,))] * 6,
            *[dma((GROUPS, AXES))] * 6,
            *[dma((AXES,))] * 2,
            dma, dma, dma((13,)), dma((13,)), dma((2, 2)), dma((2,)),
        ],
        compiler_params=pltpu.CompilerParams(
            collective_id=0, has_side_effects=True, vmem_limit_bytes=64 * 2**20
        ),
        name="expert_backward",
    )(tokens, out_grad, router_logits, expert_picks.T, micro_batch.reshape(1, T), w_gate[0], w_up[0], w_down[0])
    grad_tokens, grad_logits, balance_grad, grad_gate, grad_up, grad_down = settle(outs)
    return grad_tokens, grad_logits, balance_grad, grad_gate[None], grad_up[None], grad_down[None]


def solution(mesh):
    rows, cube = P(("dp", "ex", "ey"), None), P(("dp", "ex", "ey"), None, None)
    return jax.shard_map(
        per_device,
        mesh=mesh,
        in_specs=(rows, rows, rows, rows, P(("dp", "ex", "ey")), cube, cube, cube),
        out_specs=(rows, rows, rows, cube, cube, cube),
        check_vma=False,
    )
```

time: 220 us -> 182 us (0.83); the launches traced: 220 us -> 179 us
  Pallas kernels: 204 us -> 178 us
  local copies, waits for them, and re-layouts: 14.8 us -> 0 us
    pallas_call x1, Pallas kernels: 204 us -> 170 us  [per_device(): pl.pallas_call(kernel, out_shape=(jax.ShapeDtypeStruct((T, D), BF16), jax...]
    unnamed x11 -> x0, local copies, waits for them, and re-layouts: 14.8 us -> none
    pallas_call x0 -> x1, Pallas kernels: none -> 8.02 us  [settle(): pl.pallas_call(settle_kernel, out_shape=tuple((jax.ShapeDtypeStruct(o.sha...]
where the time goes in v2:
time: 182 us; the launch traced here: 179 us
  Pallas kernels  178 us (98%)
    pallas_call x1, Pallas kernels, per_device(): pl.pallas_call(kernel, out_shape=(jax.ShapeDtypeStruct((T, D), BF16), jax...  170 us
    pallas_call x1, Pallas kernels, settle(): pl.pallas_call(settle_kernel, out_shape=tuple((jax.ShapeDtypeStruct(o.sha...  8.02 us

profile of v2, /device:TPU:1, one launch (start us, length us, event | category | flops | bytes accessed | tf_op | source)
XLA Modules:
  0.0 178.6 jit_solution(3864251146248943922)
XLA Ops:
  0.6 169.8 %expert_backward.1 = (bf16[128,2048]{1,0:T(8,128)(2,1)}, f32[128,128]{1,0:T(8,128)}, f32[128,128]{1,0:T(8,128)}, bf16[2048,768]{1,0:T(8,128)(2,1)}, bf16[2048,76...) custom-call(bf16[128,2048]{1,0:T(8,128)(2,1)} %tok_hbm.1, bf16[128,2048]{1,0:T(8,128)(2,1)} %cot_hbm.1, f32[128,128]{1,0:T(8,128)} %logit_ref.1, ...), custom_call_target="tpu_custom_call" | custom-call | tf_op jit(solution)/shard_map/expert_backward/pallas_call | solution.py:514
  170.4 8.0 %settle.1 = (bf16[128,2048]{1,0:T(8,128)(2,1)}, f32[128,128]{1,0:T(8,128)}, f32[128,128]{1,0:T(8,128)}, bf16[2048,768]{1,0:T(8,128)(2,1)}, bf16[2048,768]{1,0:T(8,128)(2,1)}, /*index=5*/bf16[768,2048]{1,0:T(8,128)(2,1)}) custom-call(bf16[128,2048]{1,0:T(8,128)(2,1)} %get-tuple-element.18.refs_0_, f32[128,128]{1,0:T(8,128)} %get-tuple-element.19.refs_1_, ...), custom_call_target="tpu_custom_call" | custom-call | tf_op jit(solution)/shard_map/settle/pallas_call | solution.py:496

commit v3 on v2

--- a/solution.py
+++ b/solution.py
@@ -47,8 +47,10 @@
     return lax.broadcasted_iota(I32, shape, dim)
 
 
-def moved(dx, dy, dz, dc, sign=1):
+def moved(steps, dc, sign=1):
     x, ex, y = lax.axis_index("dp"), lax.axis_index("ex"), lax.axis_index("ey")
+    side = ex % 2 if sign == 1 else (ex + dc) % 2
+    dx, dy, dz = axes_of(steps, side)
     return (
         (x + sign * dx + 4) % 4,
         (ex // 2 + sign * dz + 4) % 4 * 2 + (ex % 2 + dc) % 2,
@@ -56,26 +58,31 @@
     )
 
 
+def axes_of(steps, side):
+    a, b, c = steps
+    return a + side * (c - a), b + side * (a - b), c + side * (b - c)
+
+
 def along(axis, step, sign=1):
-    return moved(*(step if axis == n else 0 for n in range(AXES)), 0, sign)
+    return moved([step if axis == n else 0 for n in range(AXES)], 0, sign)
 
 
 def in_plane(axis, j, sign=1):
     core, high, low = j // 16, (j // 4) % 4, j % 4
-    place = ((0, low, high), (low, 0, high), (low, high, 0))[axis]
-    return moved(*place, core, sign)
+    return moved(((0, low, high), (low, 0, high), (low, high, 0))[axis], core, sign)
 
 
 def any_offset(i, sign=1):
-    return moved(i % 4, (i // 4) % 4, (i // 16) % 4, i // 64, sign)
+    return moved((i % 4, (i // 4) % 4, (i // 16) % 4), i // 64, sign)
 
 
 def turn(n):
     return (n % 4 + n // 4) % 4 * 4 + n % 4
 
 
-def expert_at(dx, dy, dz, dc):
+def expert_at(steps, dc):
     x, ex, y = lax.axis_index("dp"), lax.axis_index("ex"), lax.axis_index("ey")
+    dx, dy, dz = axes_of(steps, ex % 2)
     return ((x + dx) & 3) * 32 + ((((ex // 2) + dz) & 3) * 2 + (((ex % 2) + dc) & 1)) * 4 + ((y + dy) & 3)
 
 
@@ -119,6 +126,12 @@
     def await_bytes(piece, sem):
         pltpu.make_async_copy(piece, piece, sem).wait()
 
+    pl.semaphore_wait(barrier, E - 1)
+    for s in (1, 3, 2):
+        for a in range(AXES):
+            home = tt[a].at[pl.ds(s * T, T)]
+            remote(tok_hbm.at[:, COLS_TOK[a]], home, gt_s.at[a], gt_r.at[a], along(a, s))
+
     expert_row = iota((E, T), 0)
     picked_t = jnp.zeros((E, T), F32)
     for k in range(K):
@@ -133,13 +146,13 @@
     earlier = (iota((T, T), 1) < iota((T, T), 0)).astype(BF16)
     code = jnp.where(picked > 0.0, mm(earlier, picked.astype(BF16), NN) + 1.0, 0.0).astype(BF16)
     row, lane = iota((E, E), 0), iota((E, E), 1)
-    perm = (expert_at(row & 3, (row >> 2) & 3, (row >> 4) & 3, row >> 6) == lane).astype(BF16)
+    perm = (expert_at((row & 3, (row >> 2) & 3, (row >> 4) & 3), row >> 6) == lane).astype(BF16)
     perm_ref[...] = perm
     code_rel[...] = mm(perm, code, NT)
     step, core, high, low = row >> 5, (row >> 4) & 1, (row >> 2) & 3, row & 3
     for a in range(AXES):
         place = ((step, low, high), (low, step, high), (low, high, step))[a]
-        perm = (expert_at(*place, core) == lane).astype(BF16)
+        perm = (expert_at(place, core) == lane).astype(BF16)
         code_a, weight_a = mm(perm, code, NT).astype(BF16), mm(perm, weight, NT).astype(BF16)
         for s in range(LINE):
             home = cw if s else cwg
@@ -147,12 +160,6 @@
             home[a, s * 64 + 32 : s * 64 + 64, :] = weight_a[s * 32 : s * 32 + 32, :]
     mb_hot = (mb_ref[...] == iota((8, T), 0)).astype(BF16)
     cnt[0:8, :] = mm(mb_hot, picked.astype(BF16), NN)
-    pl.semaphore_wait(barrier, E - 1)
-
-    for s in (1, 3, 2):
-        for a in range(AXES):
-            home = tt[a].at[pl.ds(s * T, T)]
-            remote(tok_hbm.at[:, COLS_TOK[a]], home, gt_s.at[a], gt_r.at[a], along(a, s))
     for s in (1, 3, 2):
         for a in range(AXES):
             piece = pl.ds(s * 64, 64)
@@ -227,15 +234,20 @@
         def _():
             dst[0 : MSG * q, :] = src[0 : MSG * q, :]
 
-    def send_group(g, parts, sign):
+    def send_groups(parts, sign):
         def send(n, carry):
-            j = g * PER + turn(n)
-            for a, (src, dst, s_sem, r_sem, q) in enumerate(parts):
+            for g, a, src, dst, s_sem, r_sem, q in parts:
+                j = g * PER + turn(n)
                 piece = rows_of(j, MSG * q)
                 remote(src.at[piece], dst.at[piece], s_sem.at[g, a], r_sem.at[g, a], in_plane(a, j, sign))
             return carry
 
-        lax.fori_loop(jnp.where(g == 0, 1, 0), PER, send, 0)
+        lax.fori_loop(1, PER, send, 0)
+        for g, a, src, dst, s_sem, r_sem, q in parts:
+            if g:
+                piece = pl.ds(g * ROWS * q, MSG * q)
+                to = in_plane(a, g * PER, sign)
+                remote(src.at[piece], dst.at[piece], s_sem.at[g, a], r_sem.at[g, a], to)
 
     def await_group(g, buf, sem, a, q):
         @pl.when(g == 0)
@@ -261,44 +273,43 @@
 
         lax.fori_loop(0, 2, half, 0)
 
-    def dispatch(g, carry):
-        part = rows_of(g, ROWS)
-        for a in range(AXES):
-
-            @pl.when(g == 0)
-            def _():
+    def find_rows(g):
+        for a in range(AXES):
+            if g == 0:
                 await_bytes(cwg.at[a, pl.ds(64, 192)], gw_r.at[a])
-
             for s in range(LINE):
                 found = mm(pick_rows(a, g, s), cwg[a, pl.ds(s * 64 + g * PER, PER), :], NN)
-                hot[a][part, s * T : (s + 1) * T] = (found == slot).astype(BF16)
-        for a in range(AXES):
-
-            @pl.when(g == 0)
-            def _():
+                hot[a][g * ROWS : (g + 1) * ROWS, s * T : (s + 1) * T] = (found == slot).astype(BF16)
+
+    def token_rows(g):
+        for a in range(AXES):
+            if g == 0:
                 await_bytes(tt[a].at[pl.ds(T, 3 * T)], gt_r.at[a])
-
-            fill(lambda rows: hot[a][rows_of(2 * g + rows, HALF), :], tt[a], Q_TOK[a])
+            fill(lambda n: hot[a][rows_of(2 * g + n, HALF), :], tt[a], Q_TOK[a])
             pack(st[a], g, Q_TOK[a])
             own_message(g, st[a], rt[a], Q_TOK[a])
-        send_group(g, [(st[a], rt[a], st_sem, rt_sem, Q_TOK[a]) for a in range(AXES)], 1)
+        return [(g, a, st[a], rt[a], st_sem, rt_sem, Q_TOK[a]) for a in range(AXES)]
+
+    def cotangent_rows(g):
         for a in range(AXES):
             for s in range(LINE):
                 lanes = slice(s * T, (s + 1) * T)
                 scale = mm(pick_rows(a, g, s), cwg[a, pl.ds(s * 64 + 32 + g * PER, PER), :], NN)
-                xs[0:ROWS, lanes] = (hot[a][part, lanes].astype(F32) * scale).astype(BF16)
-
-            @pl.when(g == 0)
-            def _():
+                one_hot = hot[a][g * ROWS : (g + 1) * ROWS, lanes].astype(F32)
+                xs[0:ROWS, lanes] = (one_hot * scale).astype(BF16)
+            if g == 0:
                 await_bytes(tc[a].at[pl.ds(T, 3 * T)], gc_r.at[a])
-
-            fill(lambda rows: xs[rows_of(rows, HALF), 0 : LINE * T], tc[a], Q_COT[a])
+            fill(lambda n: xs[rows_of(n, HALF), 0 : LINE * T], tc[a], Q_COT[a])
             pack(sc[a], g, Q_COT[a])
             own_message(g, sc[a], rc[a], Q_COT[a])
-        send_group(g, [(sc[a], rc[a], sc_sem, rc_sem, Q_COT[a]) for a in range(AXES)], 1)
-        return carry
-
-    lax.fori_loop(0, GROUPS, dispatch, 0)
+        return [(g, a, sc[a], rc[a], sc_sem, rc_sem, Q_COT[a]) for a in range(AXES)]
+
+    find_rows(0)
+    send_groups(token_rows(0), 1)
+    send_groups(cotangent_rows(0), 1)
+    find_rows(1)
+    send_groups(token_rows(1), 1)
+    send_groups(cotangent_rows(1), 1)
     count_sum(copies, 0, 0)
     copies = count_round(3, 3, 1)
     for load in loads:
@@ -317,36 +328,56 @@
     collect = (iota((2 * PER, HALF), 1) // CAP == iota((2 * PER, HALF), 0)).astype(BF16)
     slot_lane = (iota((HALF, 128), 0) % CAP == iota((HALF, 128), 1)).astype(F32)
 
+    def arrive(g, out, src, sem, chunks, cols):
+        for a in range(AXES):
+            await_group(g, src[a], sem, a, chunks[a])
+            unpack(src[a], g, chunks[a], pg, 0)
+            reorder(a, lambda lanes: pg[:, lanes], 0, out, rows_of(g, ROWS), cols[a].start, chunks[a], NN)
+
+    def send_back(g):
+        send_groups([(g, a, ps[a], pr[a], ps_sem, pr_sem, Q_PAIR[a]) for a in range(AXES)], -1)
+
+        def send_score(i, carry):
+            remote(qs.at[pl.ds(i, 1)], qr.at[pl.ds(i, 1)], qs_sem, qr_sem, any_offset(i, -1))
+            return carry
+
+        lax.fori_loop(jnp.where(g == 0, 1, g * 4 * PER), (g + 1) * 4 * PER, send_score, 0)
+
     def expert(g, carry):
-        part = rows_of(g, ROWS)
-        for out, src, sem, chunks, cols in ((xs, rt, rt_sem, Q_TOK, COLS_TOK), (cs, rc, rc_sem, Q_COT, COLS_COT)):
-            for a in range(AXES):
-                await_group(g, src[a], sem, a, chunks[a])
-                unpack(src[a], g, chunks[a], pg, 0)
-                reorder(a, lambda lanes: pg[:, lanes], 0, out, part, cols[a].start, chunks[a], NN)
-
-        def hidden_rows(n, carry):
+        arrive(g, xs, rt, rt_sem, Q_TOK, COLS_TOK)
+
+        def forward(n, carry):
             part = rows_of(2 * g + n, HALF)
-            score = jnp.zeros((HALF, 1), F32)
             for h in range(H // 256):
                 cols = slice(h * 256, (h + 1) * 256)
                 pre_gate = mm(xs[part, :], wg[:, cols], NN)
                 pre_up = mm(xs[part, :], wu[:, cols], NN)
-                back = mm(cs[part, :], wd[cols, :], NT)
                 logistic = jax.nn.sigmoid(pre_gate)
                 act = pre_gate * logistic
                 deriv = logistic * (1.0 + pre_gate * (1.0 - logistic))
-                hidden = (act * pre_up).astype(BF16)
-                hid[part, cols] = hidden
-                score = score + jnp.sum(hidden.astype(F32) * back, axis=1, keepdims=True)
-                gu[part, cols] = (back * pre_up * deriv).astype(BF16)
-                gu[part, h * 256 + H : (h + 1) * 256 + H] = (back * act).astype(BF16)
+                hid[part, cols] = (act * pre_up).astype(BF16)
+                gu[part, cols] = (pre_up * deriv).astype(BF16)
+                gu[part, h * 256 + H : (h + 1) * 256 + H] = act.astype(BF16)
+            return carry
+
+        lax.fori_loop(0, 2, forward, 0)
+        arrive(g, cs, rc, rc_sem, Q_COT, COLS_COT)
+        def backward(n, carry):
+            part = rows_of(2 * g + n, HALF)
+            score = jnp.zeros((HALF, 1), F32)
+            for h in range(H // 256):
+                cols, more = slice(h * 256, (h + 1) * 256), slice(h * 256 + H, (h + 1) * 256 + H)
+                back = mm(cs[part, :], wd[cols, :], NT)
+                score = score + jnp.sum(hid[part, cols].astype(F32) * back, axis=1, keepdims=True)
+                gu[part, cols] = (back * gu[part, cols].astype(F32)).astype(BF16)
+                gu[part, more] = (back * gu[part, more].astype(F32)).astype(BF16)
             score_rows = mm(collect, (score * slot_lane).astype(BF16), NN)
             for i in range(2 * PER):
                 qs[(2 * g + n) * 2 * PER + i] = score_rows[i : i + 1, :]
             return carry
 
-        lax.fori_loop(0, 2, hidden_rows, 0)
+        lax.fori_loop(0, 2, backward, 0)
+        part = rows_of(g, ROWS)
         for a in range(AXES):
             q, first = Q_PAIR[a], COLS_PAIR[a].start
 
@@ -358,19 +389,19 @@
             await_group(g, st[PAIR_HOME[a]], st_sem, PAIR_HOME[a], q)
             pack(ps[a], g, q)
             own_message(g, ps[a], pr[a], q)
-        send_group(g, [(ps[a], pr[a], ps_sem, pr_sem, Q_PAIR[a]) for a in range(AXES)], -1)
+
         @pl.when(g == 0)
         def _():
             qr[0] = qs[0]
 
-        def send_score(i, carry):
-            remote(qs.at[pl.ds(i, 1)], qr.at[pl.ds(i, 1)], qs_sem, qr_sem, any_offset(i, -1))
-            return carry
-
-        lax.fori_loop(jnp.where(g == 0, 1, g * 4 * PER), (g + 1) * 4 * PER, send_score, 0)
+        @pl.when(g == 0)
+        def _():
+            send_back(0)
+
         return carry
 
     lax.fori_loop(0, GROUPS, expert, 0)
+    send_back(1)
     count_sum(copies, 3, 1)
     copies = count_round(6, 7, 2)
 

time: 182 us -> 173 us (0.951); the launches traced: 179 us -> 172 us
  Pallas kernels: 178 us -> 172 us
    pallas_call x1, Pallas kernels: 170 us -> 164 us  [per_device(): pl.pallas_call(kernel, out_shape=(jax.ShapeDtypeStruct((T, D), BF16), jax...]
where the time goes in v3:
time: 173 us; the launch traced here: 172 us
  Pallas kernels  172 us (99%)
    pallas_call x1, Pallas kernels, per_device(): pl.pallas_call(kernel, out_shape=(jax.ShapeDtypeStruct((T, D), BF16), jax...  164 us
    pallas_call x1, Pallas kernels, settle(): pl.pallas_call(settle_kernel, out_shape=tuple((jax.ShapeDtypeStruct(o.sha...  8.02 us

profile of v3, /device:TPU:1, one launch (start us, length us, event | category | flops | bytes accessed | tf_op | source)
XLA Modules:
  0.0 172.5 jit_solution(17915793399087263569)
XLA Ops:
  0.6 163.7 %expert_backward.1 = (bf16[128,2048]{1,0:T(8,128)(2,1)}, f32[128,128]{1,0:T(8,128)}, f32[128,128]{1,0:T(8,128)}, bf16[2048,768]{1,0:T(8,128)(2,1)}, bf16[2048,76...) custom-call(bf16[128,2048]{1,0:T(8,128)(2,1)} %tok_hbm.1, bf16[128,2048]{1,0:T(8,128)(2,1)} %cot_hbm.1, f32[128,128]{1,0:T(8,128)} %logit_ref.1, ...), custom_call_target="tpu_custom_call" | custom-call | tf_op jit(solution)/shard_map/expert_backward/pallas_call | solution.py:545
  164.3 8.0 %settle.1 = (bf16[128,2048]{1,0:T(8,128)(2,1)}, f32[128,128]{1,0:T(8,128)}, f32[128,128]{1,0:T(8,128)}, bf16[2048,768]{1,0:T(8,128)(2,1)}, bf16[2048,768]{1,0:T(8,128)(2,1)}, /*index=5*/bf16[768,2048]{1,0:T(8,128)(2,1)}) custom-call(bf16[128,2048]{1,0:T(8,128)(2,1)} %get-tuple-element.18.refs_0_, f32[128,128]{1,0:T(8,128)} %get-tuple-element.19.refs_1_, ...), custom_call_target="tpu_custom_call" | custom-call | tf_op jit(solution)/shard_map/settle/pallas_call | solution.py:527

commit v4 on v3

--- a/solution.py
+++ b/solution.py
@@ -47,15 +47,22 @@
     return lax.broadcasted_iota(I32, shape, dim)
 
 
+def rem(value, size):
+    return lax.rem(value, jnp.int32(size)) if isinstance(value, jax.Array) else value % size
+
+
+def quot(value, size):
+    return lax.div(value, jnp.int32(size)) if isinstance(value, jax.Array) else value // size
+
+
 def moved(steps, dc, sign=1):
     x, ex, y = lax.axis_index("dp"), lax.axis_index("ex"), lax.axis_index("ey")
-    side = ex % 2 if sign == 1 else (ex + dc) % 2
+    z, core = quot(ex, 2), rem(ex, 2)
+    side = core if sign == 1 else rem(core + dc, 2)
     dx, dy, dz = axes_of(steps, side)
-    return (
-        (x + sign * dx + 4) % 4,
-        (ex // 2 + sign * dz + 4) % 4 * 2 + (ex % 2 + dc) % 2,
-        (y + sign * dy + 4) % 4,
-    )
+    if sign == -1:
+        dx, dy, dz = 4 - dx, 4 - dy, 4 - dz
+    return rem(x + dx, 4), rem(z + dz, 4) * 2 + rem(core + dc, 2), rem(y + dy, 4)
 
 
 def axes_of(steps, side):
@@ -68,16 +75,16 @@
 
 
 def in_plane(axis, j, sign=1):
-    core, high, low = j // 16, (j // 4) % 4, j % 4
+    core, high, low = quot(j, 16), rem(quot(j, 4), 4), rem(j, 4)
     return moved(((0, low, high), (low, 0, high), (low, high, 0))[axis], core, sign)
 
 
 def any_offset(i, sign=1):
-    return moved((i % 4, (i // 4) % 4, (i // 16) % 4), i // 64, sign)
+    return moved((rem(i, 4), rem(quot(i, 4), 4), rem(quot(i, 16), 4)), quot(i, 64), sign)
 
 
 def turn(n):
-    return (n % 4 + n // 4) % 4 * 4 + n % 4
+    return rem(rem(n, 4) + quot(n, 4), 4) * 4 + rem(n, 4)
 
 
 def expert_at(steps, dc):
@@ -102,11 +109,19 @@
     fs = tuple(tt[n] for n in PAIR_HOME)
     barrier = pltpu.get_barrier_semaphore()
 
-    def greet(i, carry):
-        pl.semaphore_signal(barrier, inc=1, device_id=any_offset(i), device_id_type=MESH)
+    ys = [rem(y + n, 4) for n in range(4)]
+    exs = [rem(quot(ex, 2) + n, 4) * 2 + c for n in range(4) for c in (rem(ex, 2), rem(ex + 1, 2))]
+
+    def greet(n, carry):
+        to_x = rem(x + n, 4)
+        for m in range(1, 32):
+            to = (to_x, exs[m // 4], ys[m % 4])
+            pl.semaphore_signal(barrier, inc=1, device_id=to, device_id_type=MESH)
         return carry
 
-    lax.fori_loop(1, E, greet, 0)
+    lax.fori_loop(0, 4, greet, 0)
+    for n in range(1, 4):
+        pl.semaphore_signal(barrier, inc=1, device_id=(rem(x + n, 4), ex, y), device_id_type=MESH)
     loads = [
         pltpu.make_async_copy(src, dst, w_sem.at[n])
         for n, (src, dst) in enumerate(((wg_hbm, wg), (wu_hbm, wu), (wd_hbm, wd)))
@@ -115,7 +130,7 @@
     for a in range(AXES):
         own.append(pltpu.make_async_copy(tok_hbm.at[:, COLS_TOK[a]], tt[a].at[pl.ds(0, T)], own_sem.at[0, a]))
         own.append(pltpu.make_async_copy(cot_hbm.at[:, COLS_COT[a]], tc[a].at[pl.ds(0, T)], own_sem.at[1, a]))
-    for load in own + loads:
+    for load in own:
         load.start()
 
     def remote(src, dst, send_sem, recv_sem, to):
@@ -127,10 +142,10 @@
         pltpu.make_async_copy(piece, piece, sem).wait()
 
     pl.semaphore_wait(barrier, E - 1)
-    for s in (1, 3, 2):
+    for s in (1, 3):
         for a in range(AXES):
             home = tt[a].at[pl.ds(s * T, T)]
-            remote(tok_hbm.at[:, COLS_TOK[a]], home, gt_s.at[a], gt_r.at[a], along(a, s))
+            remote(tok_hbm.at[:, COLS_TOK[a]], home, gt_s.at[a], gt_r.at[a, s], along(a, s))
 
     expert_row = iota((E, T), 0)
     picked_t = jnp.zeros((E, T), F32)
@@ -164,10 +179,21 @@
         for a in range(AXES):
             piece = pl.ds(s * 64, 64)
             remote(cw.at[a, piece], cwg.at[a, piece], gw_s.at[a], gw_r.at[a], along(a, s))
-    for s in (1, 3, 2):
+    for s in (1, 3):
         for a in range(AXES):
             home = tc[a].at[pl.ds(s * T, T)]
-            remote(cot_hbm.at[:, COLS_COT[a]], home, gc_s.at[a], gc_r.at[a], along(a, s))
+            remote(cot_hbm.at[:, COLS_COT[a]], home, gc_s.at[a], gc_r.at[a, s], along(a, s))
+
+    def pass_on(held, send_sem, recv_sem, chunks):
+        for s, begin in ((1, 0), (3, 1)):
+            for a in range(AXES):
+                await_bytes(held[a].at[pl.ds(s * T, T)], recv_sem.at[a, s])
+                lanes = pl.ds(begin * chunks[a] * 64, chunks[a] * 64)
+                block, home = held[a].at[pl.ds(s * T, T), lanes], held[a].at[pl.ds(2 * T, T), lanes]
+                remote(block, home, send_sem.at[a], recv_sem.at[a, 2], along(a, s))
+
+    for load in loads:
+        load.start()
 
     def count_round(base, others, stage):
         copies = []
@@ -284,7 +310,7 @@
     def token_rows(g):
         for a in range(AXES):
             if g == 0:
-                await_bytes(tt[a].at[pl.ds(T, 3 * T)], gt_r.at[a])
+                await_bytes(tt[a].at[pl.ds(2 * T, T)], gt_r.at[a, 2])
             fill(lambda n: hot[a][rows_of(2 * g + n, HALF), :], tt[a], Q_TOK[a])
             pack(st[a], g, Q_TOK[a])
             own_message(g, st[a], rt[a], Q_TOK[a])
@@ -298,14 +324,17 @@
                 one_hot = hot[a][g * ROWS : (g + 1) * ROWS, lanes].astype(F32)
                 xs[0:ROWS, lanes] = (one_hot * scale).astype(BF16)
             if g == 0:
-                await_bytes(tc[a].at[pl.ds(T, 3 * T)], gc_r.at[a])
+                await_bytes(tc[a].at[pl.ds(2 * T, T)], gc_r.at[a, 2])
             fill(lambda n: xs[rows_of(n, HALF), 0 : LINE * T], tc[a], Q_COT[a])
             pack(sc[a], g, Q_COT[a])
             own_message(g, sc[a], rc[a], Q_COT[a])
         return [(g, a, sc[a], rc[a], sc_sem, rc_sem, Q_COT[a]) for a in range(AXES)]
 
+    pass_on(tt, gt_s, gt_r, Q_TOK)
     find_rows(0)
-    send_groups(token_rows(0), 1)
+    parts = token_rows(0)
+    pass_on(tc, gc_s, gc_r, Q_COT)
+    send_groups(parts, 1)
     send_groups(cotangent_rows(0), 1)
     find_rows(1)
     send_groups(token_rows(1), 1)
@@ -334,14 +363,9 @@
             unpack(src[a], g, chunks[a], pg, 0)
             reorder(a, lambda lanes: pg[:, lanes], 0, out, rows_of(g, ROWS), cols[a].start, chunks[a], NN)
 
-    def send_back(g):
-        send_groups([(g, a, ps[a], pr[a], ps_sem, pr_sem, Q_PAIR[a]) for a in range(AXES)], -1)
-
-        def send_score(i, carry):
-            remote(qs.at[pl.ds(i, 1)], qr.at[pl.ds(i, 1)], qs_sem, qr_sem, any_offset(i, -1))
-            return carry
-
-        lax.fori_loop(jnp.where(g == 0, 1, g * 4 * PER), (g + 1) * 4 * PER, send_score, 0)
+    def send_score(i, carry):
+        remote(qs.at[pl.ds(i, 1)], qr.at[pl.ds(i, 1)], qs_sem, qr_sem, any_offset(i, -1))
+        return carry
 
     def expert(g, carry):
         arrive(g, xs, rt, rt_sem, Q_TOK, COLS_TOK)
@@ -378,7 +402,7 @@
 
         lax.fori_loop(0, 2, backward, 0)
         part = rows_of(g, ROWS)
-        for a in range(AXES):
+        for a in (1, 2, 0):
             q, first = Q_PAIR[a], COLS_PAIR[a].start
 
             def pair_cols(lanes):
@@ -390,18 +414,22 @@
             pack(ps[a], g, q)
             own_message(g, ps[a], pr[a], q)
 
+            def send(n, carry):
+                j = g * PER + turn(n)
+                piece = rows_of(j, MSG * q)
+                remote(ps[a].at[piece], pr[a].at[piece], ps_sem.at[g, a], pr_sem.at[g, a], in_plane(a, j, -1))
+                return carry
+
+            lax.fori_loop(jnp.where(g == 0, 1, 0), PER, send, 0)
+
         @pl.when(g == 0)
         def _():
             qr[0] = qs[0]
 
-        @pl.when(g == 0)
-        def _():
-            send_back(0)
-
+        lax.fori_loop(jnp.where(g == 0, 1, g * 4 * PER), (g + 1) * 4 * PER, send_score, 0)
         return carry
 
     lax.fori_loop(0, GROUPS, expert, 0)
-    send_back(1)
     count_sum(copies, 3, 1)
     copies = count_round(6, 7, 2)
 
@@ -437,6 +465,8 @@
         for g in range(GROUPS):
             await_group(g, pr[a], pr_sem, a, q)
             unpack(pr[a], g, q, xs, g)
+        home = PAIR_HOME[a]
+        await_bytes(tt[home].at[pl.ds(T, 3 * T)], gt_s.at[home])
         for c in range(0, q, 4):
             lanes = slice(c * 128, (c + 4) * 128)
             fs[a][:, lanes] = mm(hot[a][...], xs[:, lanes], TN).astype(BF16)
@@ -488,7 +518,6 @@
     for n in (H // 128 - 2, H // 128 - 1):
         down_copy(n, n % 2).wait()
     for a in range(AXES):
-        await_bytes(tt[a].at[pl.ds(T, 3 * T)], gt_s.at[a])
         await_bytes(tc[a].at[pl.ds(T, 3 * T)], gc_s.at[a])
         await_bytes(cw.at[a, pl.ds(64, 192)], gw_s.at[a])
         await_bytes(fr[a], fs_sem.at[a])
@@ -581,7 +610,7 @@
             pltpu.VMEM((13 * 8, E), F32),
             dma((3,)),
             dma((2, AXES)),
-            *[dma((AXES,))] * 6,
+            dma((AXES,)), dma((AXES, LINE)), dma((AXES,)), dma((AXES, LINE)), dma((AXES,)), dma((AXES,)),
             *[dma((GROUPS, AXES))] * 6,
             *[dma((AXES,))] * 2,
             dma, dma, dma((13,)), dma((13,)), dma((2, 2)), dma((2,)),

time: 173 us -> 165 us (0.954)
  Pallas kernels: 172 us -> 164 us
    pallas_call x1, Pallas kernels: 164 us -> 156 us  [per_device(): pl.pallas_call(kernel, out_shape=(jax.ShapeDtypeStruct((T, D), BF16), jax...]
where the time goes in v4:
time: 165 us
  Pallas kernels  164 us (99%)
    pallas_call x1, Pallas kernels, per_device(): pl.pallas_call(kernel, out_shape=(jax.ShapeDtypeStruct((T, D), BF16), jax...  156 us
    pallas_call x1, Pallas kernels, settle(): pl.pallas_call(settle_kernel, out_shape=tuple((jax.ShapeDtypeStruct(o.sha...  8.02 us

profile of v4, /device:TPU:1, one launch (start us, length us, event | category | flops | bytes accessed | tf_op | source)
XLA Modules:
  0.0 165.2 jit_solution(12631637611336197431)
XLA Ops:
  0.6 156.3 %expert_backward.1 = (bf16[128,2048]{1,0:T(8,128)(2,1)}, f32[128,128]{1,0:T(8,128)}, f32[128,128]{1,0:T(8,128)}, bf16[2048,768]{1,0:T(8,128)(2,1)}, bf16[2048,76...) custom-call(bf16[128,2048]{1,0:T(8,128)(2,1)} %tok_hbm.1, bf16[128,2048]{1,0:T(8,128)(2,1)} %cot_hbm.1, f32[128,128]{1,0:T(8,128)} %logit_ref.1, ...), custom_call_target="tpu_custom_call" | custom-call | tf_op jit(solution)/shard_map/expert_backward/pallas_call | solution.py:574
  157.0 8.0 %settle.1 = (bf16[128,2048]{1,0:T(8,128)(2,1)}, f32[128,128]{1,0:T(8,128)}, f32[128,128]{1,0:T(8,128)}, bf16[2048,768]{1,0:T(8,128)(2,1)}, bf16[2048,768]{1,0:T(8,128)(2,1)}, /*index=5*/bf16[768,2048]{1,0:T(8,128)(2,1)}) custom-call(bf16[128,2048]{1,0:T(8,128)(2,1)} %get-tuple-element.18.refs_0_, f32[128,128]{1,0:T(8,128)} %get-tuple-element.19.refs_1_, ...), custom_call_target="tpu_custom_call" | custom-call | tf_op jit(solution)/shard_map/settle/pallas_call | solution.py:556

commit v5 on v4

--- a/solution.py
+++ b/solution.py
@@ -226,31 +226,21 @@
 
     copies = count_round(0, 3, 0)
 
-
-    def order_block(n, carry):
-        pair = iota((64, 1), 0) + n * 64
-        s_, x_, y_, z_ = pair % CAP, pair // 9 % 4, pair // 36 % 4, pair // 144
-        perm_z[rows_of(n, 64), :] = (((y_ * 4 + x_) * 4 + z_) * CAP + s_ == iota((64, ROWS), 1)).astype(BF16)
-        return carry
-
-    lax.fori_loop(0, ROWS // 64, order_block, 0)
-    pair = iota((SHEET, 1), 0)
-    perm_y[...] = ((pair // 9 % 4 * 4 + pair // 36) * CAP + pair % CAP == iota((SHEET, SHEET), 1)).astype(BF16)
     for load in own:
         load.wait()
 
-    def pack(out, g, q):
+    def pack(out, g, q, begin=0, end=ROWS // BLK):
         def block(n, carry):
             tile = pg[rows_of(n, BLK), 0 : q * 128].reshape(BLK, q, 128)
             out[rows_of(g * (ROWS // BLK) + n, BLK * q), :] = tile.reshape(BLK * q, 128)
             return carry
 
-        lax.fori_loop(0, ROWS // BLK, block, 0)
-
-    def unpack(src, g, q, out, out_g):
+        lax.fori_loop(begin, end, block, 0)
+
+    def unpack(src, g, q, out, out_g, first=0):
         def block(n, carry):
             tile = src[rows_of(g * (ROWS // BLK) + n, BLK * q), :].reshape(BLK, q, 128)
-            out[rows_of(out_g * (ROWS // BLK) + n, BLK), 0 : q * 128] = tile.reshape(BLK, q * 128)
+            out[rows_of(out_g * (ROWS // BLK) + n, BLK), first : first + q * 128] = tile.reshape(BLK, q * 128)
             return carry
 
         lax.fori_loop(0, ROWS // BLK, block, 0)
@@ -314,7 +304,7 @@
             fill(lambda n: hot[a][rows_of(2 * g + n, HALF), :], tt[a], Q_TOK[a])
             pack(st[a], g, Q_TOK[a])
             own_message(g, st[a], rt[a], Q_TOK[a])
-        return [(g, a, st[a], rt[a], st_sem, rt_sem, Q_TOK[a]) for a in range(AXES)]
+            yield g, a, st[a], rt[a], st_sem, rt_sem, Q_TOK[a]
 
     def cotangent_rows(g):
         for a in range(AXES):
@@ -332,13 +322,23 @@
 
     pass_on(tt, gt_s, gt_r, Q_TOK)
     find_rows(0)
-    parts = token_rows(0)
     pass_on(tc, gc_s, gc_r, Q_COT)
-    send_groups(parts, 1)
+    for part in token_rows(0):
+        send_groups([part], 1)
     send_groups(cotangent_rows(0), 1)
     find_rows(1)
-    send_groups(token_rows(1), 1)
+    send_groups(list(token_rows(1)), 1)
     send_groups(cotangent_rows(1), 1)
+
+    def order_block(n, carry):
+        pair = iota((64, 1), 0) + n * 64
+        s_, x_, y_, z_ = pair % CAP, pair // 9 % 4, pair // 36 % 4, pair // 144
+        perm_z[rows_of(n, 64), :] = (((y_ * 4 + x_) * 4 + z_) * CAP + s_ == iota((64, ROWS), 1)).astype(BF16)
+        return carry
+
+    lax.fori_loop(0, ROWS // 64, order_block, 0)
+    pair = iota((SHEET, 1), 0)
+    perm_y[...] = ((pair // 9 % 4 * 4 + pair // 36) * CAP + pair % CAP == iota((SHEET, SHEET), 1)).astype(BF16)
     count_sum(copies, 0, 0)
     copies = count_round(3, 3, 1)
     for load in loads:
@@ -366,6 +366,17 @@
     def send_score(i, carry):
         remote(qs.at[pl.ds(i, 1)], qr.at[pl.ds(i, 1)], qs_sem, qr_sem, any_offset(i, -1))
         return carry
+
+    def send_last(g):
+        def send(n, carry):
+            j = g * PER + turn(n)
+            piece = rows_of(j, MSG * Q_PAIR[2])
+            remote(ps[2].at[piece], pr[2].at[piece], ps_sem.at[g, 2], pr_sem.at[g, 2], in_plane(2, j, -1))
+            return carry
+
+        lax.fori_loop(1, PER, send, 0, unroll=5)
+        if g:
+            send(0, 0)
 
     def expert(g, carry):
         arrive(g, xs, rt, rt_sem, Q_TOK, COLS_TOK)
@@ -386,6 +397,21 @@
 
         lax.fori_loop(0, 2, forward, 0)
         arrive(g, cs, rc, rc_sem, Q_COT, COLS_COT)
+        @pl.when(g == 1)
+        def _():
+            send_last(0)
+
+        for a in range(AXES):
+            await_group(g, st[PAIR_HOME[a]], st_sem, PAIR_HOME[a], Q_PAIR[a])
+
+        def pair_rows(part, lanes):
+            rows = mm(gu[part, 0:H], wg[lanes, :], NT) + mm(gu[part, H : 2 * H], wu[lanes, :], NT)
+            return rows.astype(BF16)
+
+        def send_pair(a, j):
+            piece = rows_of(j, MSG * Q_PAIR[a])
+            remote(ps[a].at[piece], pr[a].at[piece], ps_sem.at[g, a], pr_sem.at[g, a], in_plane(a, j, -1))
+
         def backward(n, carry):
             part = rows_of(2 * g + n, HALF)
             score = jnp.zeros((HALF, 1), F32)
@@ -395,6 +421,28 @@
                 score = score + jnp.sum(hid[part, cols].astype(F32) * back, axis=1, keepdims=True)
                 gu[part, cols] = (back * gu[part, cols].astype(F32)).astype(BF16)
                 gu[part, more] = (back * gu[part, more].astype(F32)).astype(BF16)
+            for a in (1, 0):
+                q, first = Q_PAIR[a], COLS_PAIR[a].start
+                for c in range(0, q * 128, 256):
+                    rows = pair_rows(part, slice(first + c, first + c + 256))
+                    if a == 1:
+                        sheets = [rows[m * SHEET : (m + 1) * SHEET, :] for m in range(HALF // SHEET)]
+                        sheets = [mm(perm_y[...], sheet, TN).astype(BF16) for sheet in sheets]
+                        rows = jnp.concatenate(sheets, axis=0)
+                    pg[rows_of(n, HALF), c : c + 256] = rows
+                pack(ps[a], g, q, n * (HALF // BLK), (n + 1) * (HALF // BLK))
+
+                @pl.when(g + n == 0)
+                def _():
+                    pr[a][0 : MSG * q, :] = ps[a][0 : MSG * q, :]
+
+                def send(m, carry):
+                    low = rem(m, 4)
+                    send_pair(a, g * PER + (2 * n + rem(low + quot(m, 4), 2)) * 4 + low)
+                    return carry
+
+                pl.when(g + n > 0)(lambda: send(0, None))
+                lax.fori_loop(1, PER // 2, send, 0, unroll=True)
             score_rows = mm(collect, (score * slot_lane).astype(BF16), NN)
             for i in range(2 * PER):
                 qs[(2 * g + n) * 2 * PER + i] = score_rows[i : i + 1, :]
@@ -402,25 +450,14 @@
 
         lax.fori_loop(0, 2, backward, 0)
         part = rows_of(g, ROWS)
-        for a in (1, 2, 0):
-            q, first = Q_PAIR[a], COLS_PAIR[a].start
-
-            def pair_cols(lanes):
-                rows = mm(gu[part, 0:H], wg[lanes, :], NT) + mm(gu[part, H : 2 * H], wu[lanes, :], NT)
-                return rows.astype(BF16)
-
-            reorder(a, pair_cols, first, pg, slice(0, ROWS), 0, q, TN)
-            await_group(g, st[PAIR_HOME[a]], st_sem, PAIR_HOME[a], q)
-            pack(ps[a], g, q)
-            own_message(g, ps[a], pr[a], q)
-
-            def send(n, carry):
-                j = g * PER + turn(n)
-                piece = rows_of(j, MSG * q)
-                remote(ps[a].at[piece], pr[a].at[piece], ps_sem.at[g, a], pr_sem.at[g, a], in_plane(a, j, -1))
-                return carry
-
-            lax.fori_loop(jnp.where(g == 0, 1, 0), PER, send, 0)
+        first = COLS_PAIR[2].start
+        reorder(2, lambda lanes: pair_rows(part, lanes), first, pg, slice(0, ROWS), 0, Q_PAIR[2], TN)
+        pack(ps[2], g, Q_PAIR[2])
+        own_message(g, ps[2], pr[2], Q_PAIR[2])
+
+        @pl.when(g == 1)
+        def _():
+            send_last(1)
 
         @pl.when(g == 0)
         def _():
@@ -461,15 +498,17 @@
             copy.wait()
 
     for a in range(AXES):
+        await_group(0, pr[a], pr_sem, a, Q_PAIR[a])
+        unpack(pr[a], 0, Q_PAIR[a], xs, 0, COLS_PAIR[a].start)
+    for a in range(AXES):
         q = Q_PAIR[a]
-        for g in range(GROUPS):
-            await_group(g, pr[a], pr_sem, a, q)
-            unpack(pr[a], g, q, xs, g)
+        await_group(1, pr[a], pr_sem, a, q)
+        unpack(pr[a], 1, q, xs, 1, COLS_PAIR[a].start)
         home = PAIR_HOME[a]
         await_bytes(tt[home].at[pl.ds(T, 3 * T)], gt_s.at[home])
         for c in range(0, q, 4):
-            lanes = slice(c * 128, (c + 4) * 128)
-            fs[a][:, lanes] = mm(hot[a][...], xs[:, lanes], TN).astype(BF16)
+            lanes, cols = slice(c * 128, (c + 4) * 128), pl.ds(COLS_PAIR[a].start + c * 128, 512)
+            fs[a][:, lanes] = mm(hot[a][...], xs[:, cols], TN).astype(BF16)
         for s in (1, 3, 2):
             piece = fr[a].at[pl.ds((s - 1) * T, T)]
             remote(fs[a].at[pl.ds(s * T, T)], piece, fs_sem.at[a], fr_sem.at[a], along(a, s, -1))

time: 165 us -> 163 us (0.988)
  Pallas kernels: 164 us -> 161 us
    pallas_call x1, Pallas kernels: 156 us -> 153 us  [per_device(): pl.pallas_call(kernel, out_shape=(jax.ShapeDtypeStruct((T, D), BF16), jax...]
where the time goes in v5:
time: 163 us; the launch traced here: 162 us
  Pallas kernels  161 us (99%)
    pallas_call x1, Pallas kernels, per_device(): pl.pallas_call(kernel, out_shape=(jax.ShapeDtypeStruct((T, D), BF16), jax...  153 us
    pallas_call x1, Pallas kernels, settle(): pl.pallas_call(settle_kernel, out_shape=tuple((jax.ShapeDtypeStruct(o.sha...  8.02 us

profile of v5, /device:TPU:1, one launch (start us, length us, event | category | flops | bytes accessed | tf_op | source)
XLA Modules:
  0.0 162.3 jit_solution(10010357395736245197)
XLA Ops:
  0.6 153.5 %expert_backward.1 = (bf16[128,2048]{1,0:T(8,128)(2,1)}, f32[128,128]{1,0:T(8,128)}, f32[128,128]{1,0:T(8,128)}, bf16[2048,768]{1,0:T(8,128)(2,1)}, bf16[2048,76...) custom-call(bf16[128,2048]{1,0:T(8,128)(2,1)} %tok_hbm.1, bf16[128,2048]{1,0:T(8,128)(2,1)} %cot_hbm.1, f32[128,128]{1,0:T(8,128)} %logit_ref.1, ...), custom_call_target="tpu_custom_call" | custom-call | tf_op jit(solution)/shard_map/expert_backward/pallas_call | solution.py:613
  154.1 8.0 %settle.1 = (bf16[128,2048]{1,0:T(8,128)(2,1)}, f32[128,128]{1,0:T(8,128)}, f32[128,128]{1,0:T(8,128)}, bf16[2048,768]{1,0:T(8,128)(2,1)}, bf16[2048,768]{1,0:T(8,128)(2,1)}, /*index=5*/bf16[768,2048]{1,0:T(8,128)(2,1)}) custom-call(bf16[128,2048]{1,0:T(8,128)(2,1)} %get-tuple-element.18.refs_0_, f32[128,128]{1,0:T(8,128)} %get-tuple-element.19.refs_1_, ...), custom_call_target="tpu_custom_call" | custom-call | tf_op jit(solution)/shard_map/settle/pallas_call | solution.py:595

commit v6 on v5

--- a/solution.py
+++ b/solution.py
@@ -396,11 +396,12 @@
             return carry
 
         lax.fori_loop(0, 2, forward, 0)
+
+        @pl.when(g == 1)
+        def _():
+            send_last(0)
+
         arrive(g, cs, rc, rc_sem, Q_COT, COLS_COT)
-        @pl.when(g == 1)
-        def _():
-            send_last(0)
-
         for a in range(AXES):
             await_group(g, st[PAIR_HOME[a]], st_sem, PAIR_HOME[a], Q_PAIR[a])
 
@@ -509,9 +510,9 @@
         for c in range(0, q, 4):
             lanes, cols = slice(c * 128, (c + 4) * 128), pl.ds(COLS_PAIR[a].start + c * 128, 512)
             fs[a][:, lanes] = mm(hot[a][...], xs[:, cols], TN).astype(BF16)
-        for s in (1, 3, 2):
-            piece = fr[a].at[pl.ds((s - 1) * T, T)]
-            remote(fs[a].at[pl.ds(s * T, T)], piece, fs_sem.at[a], fr_sem.at[a], along(a, s, -1))
+            for s in (2, 1, 3):
+                home = fr[a].at[pl.ds((s - 1) * T, T), lanes]
+                remote(fs[a].at[pl.ds(s * T, T), lanes], home, fs_sem.at[a], fr_sem.at[a], along(a, s, -1))
 
     def down_copy(n, buf):
         place = gd_hbm.at[rows_of(n // 2, 256), rows_of(n % 2, D // 2)]

time: 163 us -> 161 us (0.988)
    pallas_call x1, Pallas kernels: 153 us -> 152 us  [per_device(): pl.pallas_call(kernel, out_shape=(jax.ShapeDtypeStruct((T, D), BF16), jax...]
where the time goes in v6:
time: 161 us
  Pallas kernels  160 us (99%)
    pallas_call x1, Pallas kernels, per_device(): pl.pallas_call(kernel, out_shape=(jax.ShapeDtypeStruct((T, D), BF16), jax...  152 us
    pallas_call x1, Pallas kernels, settle(): pl.pallas_call(settle_kernel, out_shape=tuple((jax.ShapeDtypeStruct(o.sha...  8.02 us

profile of v6, /device:TPU:1, one launch (start us, length us, event | category | flops | bytes accessed | tf_op | source)
XLA Modules:
  0.0 160.5 jit_solution(13961077150146033891)
XLA Ops:
  0.6 151.7 %expert_backward.1 = (bf16[128,2048]{1,0:T(8,128)(2,1)}, f32[128,128]{1,0:T(8,128)}, f32[128,128]{1,0:T(8,128)}, bf16[2048,768]{1,0:T(8,128)(2,1)}, bf16[2048,76...) custom-call(bf16[128,2048]{1,0:T(8,128)(2,1)} %tok_hbm.1, bf16[128,2048]{1,0:T(8,128)(2,1)} %cot_hbm.1, f32[128,128]{1,0:T(8,128)} %logit_ref.1, ...), custom_call_target="tpu_custom_call" | custom-call | tf_op jit(solution)/shard_map/expert_backward/pallas_call | solution.py:614
  152.4 8.0 %settle.1 = (bf16[128,2048]{1,0:T(8,128)(2,1)}, f32[128,128]{1,0:T(8,128)}, f32[128,128]{1,0:T(8,128)}, bf16[2048,768]{1,0:T(8,128)(2,1)}, bf16[2048,768]{1,0:T(8,128)(2,1)}, /*index=5*/bf16[768,2048]{1,0:T(8,128)(2,1)}) custom-call(bf16[128,2048]{1,0:T(8,128)(2,1)} %get-tuple-element.18.refs_0_, f32[128,128]{1,0:T(8,128)} %get-tuple-element.19.refs_1_, ...), custom_call_target="tpu_custom_call" | custom-call | tf_op jit(solution)/shard_map/settle/pallas_call | solution.py:596

commit v7 on v6

--- a/solution.py
+++ b/solution.py
@@ -99,7 +99,7 @@
     st0, st1, st2, sc0, sc1, sc2, rt0, rt1, rt2, rc0, rc1, rc2, pr0, pr1, pr2,
     tt0, tt1, tt2, tc0, tc1, tc2, hot0, hot1, hot2, fr0, fr1, fr2, perm_y, perm_z,
     xs, cs, hid, gu, wg, wu, wd, pg, out_buf, cw, cwg, code_rel, perm_ref, rwm_ref, qs, qr, cnt, cnt_in,
-    w_sem, own_sem, gt_s, gt_r, gc_s, gc_r, gw_s, gw_r, st_sem, sc_sem, rt_sem, rc_sem, ps_sem, pr_sem, fs_sem, fr_sem,
+    w_sem, own_sem, gt_s, gt_r, gh_r, gc_s, gc_r, gw_s, gw_r, st_sem, sc_sem, rt_sem, rc_sem, ps_sem, pr_sem, fs_sem, fr_sem,
     qs_sem, qr_sem, cs_sem, cr_sem, oa_sem, od_sem,
 ):
     x, ex, y = lax.axis_index("dp"), lax.axis_index("ex"), lax.axis_index("ey")
@@ -142,10 +142,14 @@
         pltpu.make_async_copy(piece, piece, sem).wait()
 
     pl.semaphore_wait(barrier, E - 1)
-    for s in (1, 3):
-        for a in range(AXES):
-            home = tt[a].at[pl.ds(s * T, T)]
-            remote(tok_hbm.at[:, COLS_TOK[a]], home, gt_s.at[a], gt_r.at[a, s], along(a, s))
+    for first in (True, False):
+        for s in (1, 3):
+            for a in range(AXES):
+                width = Q_TOK[a] * 64
+                begin = width if (s == 3) == first else 0
+                block = tok_hbm.at[:, pl.ds(COLS_TOK[a].start + begin, width)]
+                home = tt[a].at[pl.ds(s * T, T), pl.ds(begin, width)]
+                remote(block, home, gt_s.at[a], (gt_r if first else gh_r).at[a, s], along(a, s))
 
     expert_row = iota((E, T), 0)
     picked_t = jnp.zeros((E, T), F32)
@@ -184,11 +188,12 @@
             home = tc[a].at[pl.ds(s * T, T)]
             remote(cot_hbm.at[:, COLS_COT[a]], home, gc_s.at[a], gc_r.at[a, s], along(a, s))
 
-    def pass_on(held, send_sem, recv_sem, chunks):
+    def pass_on(held, send_sem, recv_sem, chunks, halves=False):
         for s, begin in ((1, 0), (3, 1)):
             for a in range(AXES):
-                await_bytes(held[a].at[pl.ds(s * T, T)], recv_sem.at[a, s])
                 lanes = pl.ds(begin * chunks[a] * 64, chunks[a] * 64)
+                whole = held[a].at[pl.ds(s * T, T)]
+                await_bytes(held[a].at[pl.ds(s * T, T), lanes] if halves else whole, recv_sem.at[a, s])
                 block, home = held[a].at[pl.ds(s * T, T), lanes], held[a].at[pl.ds(2 * T, T), lanes]
                 remote(block, home, send_sem.at[a], recv_sem.at[a, 2], along(a, s))
 
@@ -258,7 +263,7 @@
                 remote(src.at[piece], dst.at[piece], s_sem.at[g, a], r_sem.at[g, a], in_plane(a, j, sign))
             return carry
 
-        lax.fori_loop(1, PER, send, 0)
+        lax.fori_loop(1, PER, send, 0, unroll=5)
         for g, a, src, dst, s_sem, r_sem, q in parts:
             if g:
                 piece = pl.ds(g * ROWS * q, MSG * q)
@@ -301,6 +306,8 @@
         for a in range(AXES):
             if g == 0:
                 await_bytes(tt[a].at[pl.ds(2 * T, T)], gt_r.at[a, 2])
+                for s, begin in ((1, Q_TOK[a] * 64), (3, 0)):
+                    await_bytes(tt[a].at[pl.ds(s * T, T), pl.ds(begin, Q_TOK[a] * 64)], gh_r.at[a, s])
             fill(lambda n: hot[a][rows_of(2 * g + n, HALF), :], tt[a], Q_TOK[a])
             pack(st[a], g, Q_TOK[a])
             own_message(g, st[a], rt[a], Q_TOK[a])
@@ -320,7 +327,7 @@
             own_message(g, sc[a], rc[a], Q_COT[a])
         return [(g, a, sc[a], rc[a], sc_sem, rc_sem, Q_COT[a]) for a in range(AXES)]
 
-    pass_on(tt, gt_s, gt_r, Q_TOK)
+    pass_on(tt, gt_s, gt_r, Q_TOK, True)
     find_rows(0)
     pass_on(tc, gc_s, gc_r, Q_COT)
     for part in token_rows(0):
@@ -650,7 +657,7 @@
             pltpu.VMEM((13 * 8, E), F32),
             dma((3,)),
             dma((2, AXES)),
-            dma((AXES,)), dma((AXES, LINE)), dma((AXES,)), dma((AXES, LINE)), dma((AXES,)), dma((AXES,)),
+            dma((AXES,)), dma((AXES, LINE)), dma((AXES, LINE)), dma((AXES,)), dma((AXES, LINE)), dma((AXES,)), dma((AXES,)),
             *[dma((GROUPS, AXES))] * 6,
             *[dma((AXES,))] * 2,
             dma, dma, dma((13,)), dma((13,)), dma((2, 2)), dma((2,)),

time: 161 us -> 162 us (level); the launches traced: 161 us -> 160 us
  no operation moved by 1% of the time
where the time goes in v7:
time: 162 us; the launch traced here: 160 us
  Pallas kernels  159 us (98%)
    pallas_call x1, Pallas kernels, per_device(): pl.pallas_call(kernel, out_shape=(jax.ShapeDtypeStruct((T, D), BF16), jax...  151 us
    pallas_call x1, Pallas kernels, settle(): pl.pallas_call(settle_kernel, out_shape=tuple((jax.ShapeDtypeStruct(o.sha...  8.02 us

profile of v7, /device:TPU:1, one launch (start us, length us, event | category | flops | bytes accessed | tf_op | source)
XLA Modules:
  0.0 159.7 jit_solution(16108366330948359461)
XLA Ops:
  0.6 150.9 %expert_backward.1 = (bf16[128,2048]{1,0:T(8,128)(2,1)}, f32[128,128]{1,0:T(8,128)}, f32[128,128]{1,0:T(8,128)}, bf16[2048,768]{1,0:T(8,128)(2,1)}, bf16[2048,76...) custom-call(bf16[128,2048]{1,0:T(8,128)(2,1)} %tok_hbm.1, bf16[128,2048]{1,0:T(8,128)(2,1)} %cot_hbm.1, f32[128,128]{1,0:T(8,128)} %logit_ref.1, ...), custom_call_target="tpu_custom_call" | custom-call | tf_op jit(solution)/shard_map/expert_backward/pallas_call | solution.py:621
  151.5 8.0 %settle.1 = (bf16[128,2048]{1,0:T(8,128)(2,1)}, f32[128,128]{1,0:T(8,128)}, f32[128,128]{1,0:T(8,128)}, bf16[2048,768]{1,0:T(8,128)(2,1)}, bf16[2048,768]{1,0:T(8,128)(2,1)}, /*index=5*/bf16[768,2048]{1,0:T(8,128)(2,1)}) custom-call(bf16[128,2048]{1,0:T(8,128)(2,1)} %get-tuple-element.18.refs_0_, f32[128,128]{1,0:T(8,128)} %get-tuple-element.19.refs_1_, ...), custom_call_target="tpu_custom_call" | custom-call | tf_op jit(solution)/shard_map/settle/pallas_call | solution.py:603
